TPU v7x, 128 devices: a whole 4x4x4 slice. The times are simulated.
128 devices in a mesh: section: 2 (over x_lo), dp: 32 (over z, x_hi, y), tensor: 2 (over core).
Axes of the slice: x: 4 (x_hi: 2, x_lo: 2; x = x_hi * 2 + x_lo), y: 4, z: 4, core: 2. Of those that a mesh axis runs over, the one named last changes fastest.
Arguments:
- block_input: bfloat16 [16384, 1024], P('dp'), may hold values from -6 to 6
- doc_lengths: int32 [64, 4], P('dp'), may hold values from 1 to 128, 256 in all within a row
- out_cotangent: bfloat16 [16384, 1024], P('dp'), may hold values from -6 to 6
- attn_gain: float32 [2, 1024], P('section'), may hold values from 0.5 to 1.5
- q_gain: float32 [2, 128], P('section'), may hold values from 0.5 to 1.5
- k_gain: float32 [2, 128], P('section'), may hold values from 0.5 to 1.5
- mlp_gain: float32 [2, 1024], P('section'), may hold values from 0.5 to 1.5
- q_weight: bfloat16 [2, 1024, 2048], P('section', None, 'tensor'), may hold values from -0.1875 to 0.1875
- key_matrix: bfloat16 [2, 1024, 1024], P('section', None, 'tensor'), may hold values from -0.1875 to 0.1875
- value_matrix: bfloat16 [2, 1024, 1024], P('section', None, 'tensor'), may hold values from -0.1875 to 0.1875
- o_weight: bfloat16 [2, 1024, 2048], P('section', None, 'tensor'), may hold values from -0.25 to 0.25
- gate_weight: bfloat16 [2, 1024, 3072], P('section', None, 'tensor'), may hold values from -0.1875 to 0.1875
- up_weight: bfloat16 [2, 1024, 3072], P('section', None, 'tensor'), may hold values from -0.1875 to 0.1875
- down_weight: bfloat16 [2, 1024, 3072], P('section', None, 'tensor'), may hold values from -0.109375 to 0.109375
Outputs:
- hidden_out: float32 [2, 16384, 1024], P('section', 'dp')
- hidden_grad: float32 [2, 16384, 1024], P('section', 'dp')
- attn_gain_grad: float32 [2, 1024], P('section')
- q_gain_grad: float32 [2, 128], P('section')
- k_gain_grad: float32 [2, 128], P('section')
- mlp_gain_grad: float32 [2, 1024], P('section')
- q_grad: float32 [2, 1024, 2048], P('section', 'dp', 'tensor')
- k_grad: float32 [2, 1024, 1024], P('section', 'dp', 'tensor')
- v_grad: float32 [2, 1024, 1024], P('section', 'dp', 'tensor')
- o_grad: float32 [2, 1024, 2048], P('section', 'dp', 'tensor')
- gate_grad: float32 [2, 1024, 3072], P('section', 'dp', 'tensor')
- up_grad: float32 [2, 1024, 3072], P('section', 'dp', 'tensor')
- down_grad: float32 [2, 1024, 3072], P('section', 'dp', 'tensor')
Inputs may be any that keep to these rules, and one draw needn't show every extreme that they name: `doc_lengths`: each row's 4 lengths sum to 256, and each row's largest is exactly 128; row m of a dp index's 2 rows is its m-th micro-batch.
All inputs are finite; a program needn't handle non-finite values.
Results may differ from a plain program's by a relative error of at most 0.03.
Values may be sent and summed in bfloat16 or wider, within the bound.
A program may use at most 192 MiB of HBM per device.

v0:
```python
import jax
import jax.numpy as jnp
from jax import lax
from jax.sharding import PartitionSpec as P

HEAD_SIZE = 128


EPSILON = 1e-06
THETA = 1000000.0
CONTRACT_ROWS = (((0,), (0,)), ((), ()))
CONTRACT_COLS = (((1,), (1,)), ((), ()))


def passed_along(shard, axis, by):
    peers = lax.axis_size(axis)
    pairs = [(i, i + by) for i in range(peers) if 0 <= i + by < peers]
    return lax.ppermute(shard, axis, pairs)


def doc_tables(lengths, rows):
    ends = jnp.cumsum(lengths, axis=-1, dtype=jnp.int32)
    starts = ends - lengths
    place = jnp.arange(rows, dtype=jnp.int32)
    inside = (place[None, :, None] >= starts[:, None, :]) & (
        place[None, :, None] < ends[:, None, :]
    )
    begins = jnp.sum(jnp.where(inside, starts[:, None, :], 0), axis=-1, dtype=jnp.int32)
    finished = jnp.sum(
        (place[None, :, None] >= ends[:, None, :]).astype(jnp.int32), axis=-1, dtype=jnp.int32
    )
    offsets = place[None, :] - begins
    allowed = (finished[:, :, None] == finished[:, None, :]) & (
        place[None, None, :] <= place[None, :, None]
    )
    return (offsets, allowed)


def rope_tables(offsets, size):
    half = size // 2
    rates = jnp.power(THETA, -2.0 * jnp.arange(half, dtype=jnp.float32) / size)
    angle = offsets.astype(jnp.float32)[..., None] * rates
    angle = jnp.concatenate([angle, angle], axis=-1)
    return (jnp.cos(angle), jnp.sin(angle))


def turn_half(value):
    half = value.shape[-1] // 2
    return jnp.concatenate([-value[..., half:], value[..., :half]], axis=-1)


def rotate(value, cosine, sine):
    return value * cosine[:, None, :] + turn_half(value) * sine[:, None, :]


def unrotate(grad, cosine, sine):
    half = grad.shape[-1] // 2
    moved = grad * sine[:, None, :]
    return grad * cosine[:, None, :] + jnp.concatenate(
        [moved[..., half:], -moved[..., :half]], axis=-1
    )


def inverse_rms(value):
    return lax.rsqrt(jnp.mean(value * value, axis=-1, keepdims=True) + EPSILON)


def norm_back(grad, value, scale, gain):
    inner = grad * gain
    return scale * inner - value * (scale * scale * scale) * jnp.mean(
        inner * value, axis=-1, keepdims=True
    )


def scores_for(rotated_query, key_rot, allowed):
    raw = jnp.einsum(
        "rkgd,ckd->kgrc", rotated_query, key_rot, preferred_element_type=jnp.float32
    ) * HEAD_SIZE ** (-0.5)
    return jnp.where(allowed[None, None], raw, -1000000000.0)


def pick(table, index):
    return lax.dynamic_index_in_dim(table, index, 0, keepdims=False)


def layer_forward(hidden, cosine, sine, allowed, weights):
    (
        attn_gain,
        q_gain,
        k_gain,
        mlp_gain,
        q_weight,
        key_matrix,
        value_matrix,
        o_weight,
        gate_weight,
        up_weight,
        down_weight,
    ) = weights
    rows = hidden.shape[0]
    heads = q_weight.shape[1] // HEAD_SIZE
    groups = key_matrix.shape[1] // HEAD_SIZE
    scale_one = inverse_rms(hidden)
    normed_input = (hidden * scale_one * attn_gain).astype(jnp.bfloat16)
    query = jnp.dot(normed_input, q_weight, preferred_element_type=jnp.float32).reshape(
        rows, heads, HEAD_SIZE
    )
    key_rows = jnp.dot(normed_input, key_matrix, preferred_element_type=jnp.float32).reshape(
        rows, groups, HEAD_SIZE
    )
    value_rows = (
        jnp.dot(normed_input, value_matrix, preferred_element_type=jnp.float32)
        .astype(jnp.bfloat16)
        .reshape(rows, groups, HEAD_SIZE)
    )
    q_scale = inverse_rms(query)
    k_scale = inverse_rms(key_rows)
    rotated_query = (
        rotate(query * q_scale * q_gain, cosine, sine)
        .astype(jnp.bfloat16)
        .reshape(rows, groups, heads // groups, HEAD_SIZE)
    )
    key_rot = rotate(key_rows * k_scale * k_gain, cosine, sine).astype(jnp.bfloat16)
    scores = scores_for(rotated_query, key_rot, allowed)
    peak = jnp.max(scores, axis=-1, keepdims=True)
    log_total = peak + jnp.log(jnp.sum(jnp.exp(scores - peak), axis=-1, keepdims=True))
    probs_low = jnp.exp(scores - log_total).astype(jnp.bfloat16)
    mixed = (
        jnp.einsum("kgrc,ckd->rkgd", probs_low, value_rows, preferred_element_type=jnp.float32)
        .reshape(rows, heads * HEAD_SIZE)
        .astype(jnp.bfloat16)
    )
    attended = lax.psum(
        lax.dot_general(mixed, o_weight, CONTRACT_COLS, preferred_element_type=jnp.float32),
        "tensor",
    )
    middle = hidden + attended
    scale_two = inverse_rms(middle)
    normed_two = (middle * scale_two * mlp_gain).astype(jnp.bfloat16)
    gate = jnp.dot(normed_two, gate_weight, preferred_element_type=jnp.float32)
    up = jnp.dot(normed_two, up_weight, preferred_element_type=jnp.float32)
    act = (jax.nn.silu(gate) * up).astype(jnp.bfloat16)
    moved = lax.psum(
        lax.dot_general(act, down_weight, CONTRACT_COLS, preferred_element_type=jnp.float32),
        "tensor",
    )
    kept = (
        hidden,
        scale_one,
        normed_input,
        query,
        q_scale,
        key_rows,
        k_scale,
        value_rows,
        rotated_query,
        key_rot,
        log_total,
        mixed,
        middle,
        scale_two,
        normed_two,
        gate,
        up,
        act,
    )
    return (middle + moved, kept)


def mlp_backward(grad_out, kept, weights):
    mlp_gain = weights[3]
    gate_weight, up_weight, down_weight = (weights[8], weights[9], weights[10])
    middle, scale_two, normed_two, gate, up, act = kept[12:18]
    moved_grad = grad_out.astype(jnp.bfloat16)
    down_term = lax.dot_general(moved_grad, act, CONTRACT_ROWS, preferred_element_type=jnp.float32)
    act_grad = jnp.dot(moved_grad, down_weight, preferred_element_type=jnp.float32)
    sigma = jax.nn.sigmoid(gate)
    gate_low = (act_grad * up * sigma * (1.0 + gate * (1.0 - sigma))).astype(jnp.bfloat16)
    up_low = (act_grad * gate * sigma).astype(jnp.bfloat16)
    gate_term = lax.dot_general(
        normed_two, gate_low, CONTRACT_ROWS, preferred_element_type=jnp.float32
    )
    up_term = lax.dot_general(normed_two, up_low, CONTRACT_ROWS, preferred_element_type=jnp.float32)
    normed_part = lax.dot_general(
        gate_low, gate_weight, CONTRACT_COLS, preferred_element_type=jnp.float32
    )
    normed_part = normed_part + lax.dot_general(
        up_low, up_weight, CONTRACT_COLS, preferred_element_type=jnp.float32
    )
    gain_part = jnp.sum(normed_part * middle * scale_two, axis=0)
    normed_grad = lax.psum(normed_part, "tensor")
    middle_grad = grad_out + norm_back(normed_grad, middle, scale_two, mlp_gain)
    return (middle_grad, gain_part, (gate_term, up_term, down_term))


def attention_backward(middle_grad, kept, cosine, sine, allowed, weights):
    attn_gain, q_gain, k_gain = (weights[0], weights[1], weights[2])
    q_weight, key_matrix, value_matrix, o_weight = (weights[4], weights[5], weights[6], weights[7])
    (
        hidden,
        scale_one,
        normed_input,
        query,
        q_scale,
        key_rows,
        k_scale,
        value_rows,
        rotated_query,
        key_rot,
        log_total,
        mixed,
    ) = kept[:12]
    rows = query.shape[0]
    heads = query.shape[1]
    groups = key_rows.shape[1]
    scale = HEAD_SIZE ** (-0.5)
    attended_grad = middle_grad.astype(jnp.bfloat16)
    o_term = lax.dot_general(
        attended_grad, mixed, CONTRACT_ROWS, preferred_element_type=jnp.float32
    )
    mixed_grad = jnp.dot(attended_grad, o_weight, preferred_element_type=jnp.float32).astype(
        jnp.bfloat16
    )
    mixed_grad = mixed_grad.reshape(rows, groups, heads // groups, HEAD_SIZE)
    probs = jnp.exp(scores_for(rotated_query, key_rot, allowed) - log_total)
    probs_low = probs.astype(jnp.bfloat16)
    probs_grad = jnp.einsum(
        "rkgd,ckd->kgrc", mixed_grad, value_rows, preferred_element_type=jnp.float32
    )
    value_grad = jnp.einsum(
        "kgrc,rkgd->ckd", probs_low, mixed_grad, preferred_element_type=jnp.float32
    )
    score_grad = (
        probs * (probs_grad - jnp.sum(probs * probs_grad, axis=-1, keepdims=True))
    ).astype(jnp.bfloat16)
    query_rot_grad = (
        jnp.einsum(
            "kgrc,ckd->rkgd", score_grad, key_rot, preferred_element_type=jnp.float32
        ).reshape(rows, heads, HEAD_SIZE)
        * scale
    )
    key_rot_grad = (
        jnp.einsum("kgrc,rkgd->ckd", score_grad, rotated_query, preferred_element_type=jnp.float32)
        * scale
    )
    query_turn = unrotate(query_rot_grad, cosine, sine)
    key_turn = unrotate(key_rot_grad, cosine, sine)
    q_gain_part = jnp.sum(query_turn * query * q_scale, axis=(0, 1))
    k_gain_part = jnp.sum(key_turn * key_rows * k_scale, axis=(0, 1))
    query_grad = (
        norm_back(query_turn, query, q_scale, q_gain)
        .reshape(rows, heads * HEAD_SIZE)
        .astype(jnp.bfloat16)
    )
    key_grad = (
        norm_back(key_turn, key_rows, k_scale, k_gain)
        .reshape(rows, groups * HEAD_SIZE)
        .astype(jnp.bfloat16)
    )
    value_low = value_grad.reshape(rows, groups * HEAD_SIZE).astype(jnp.bfloat16)
    q_term = lax.dot_general(
        normed_input, query_grad, CONTRACT_ROWS, preferred_element_type=jnp.float32
    )
    k_term = lax.dot_general(
        normed_input, key_grad, CONTRACT_ROWS, preferred_element_type=jnp.float32
    )
    v_term = lax.dot_general(
        normed_input, value_low, CONTRACT_ROWS, preferred_element_type=jnp.float32
    )
    normed_part = lax.dot_general(
        query_grad, q_weight, CONTRACT_COLS, preferred_element_type=jnp.float32
    )
    normed_part = normed_part + lax.dot_general(
        key_grad, key_matrix, CONTRACT_COLS, preferred_element_type=jnp.float32
    )
    normed_part = normed_part + lax.dot_general(
        value_low, value_matrix, CONTRACT_COLS, preferred_element_type=jnp.float32
    )
    attn_gain_part = jnp.sum(normed_part * hidden * scale_one, axis=0)
    normed_grad = lax.psum(normed_part, "tensor")
    grad_in = middle_grad + norm_back(normed_grad, hidden, scale_one, attn_gain)
    return (grad_in, (attn_gain_part, q_gain_part, k_gain_part), (q_term, k_term, v_term, o_term))


def shards(
    block_input,
    doc_lengths,
    out_cotangent,
    attn_gain,
    q_gain,
    k_gain,
    mlp_gain,
    q_weight,
    key_matrix,
    value_matrix,
    o_weight,
    gate_weight,
    up_weight,
    down_weight,
):
    weights = (
        attn_gain[0],
        q_gain[0],
        k_gain[0],
        mlp_gain[0],
        q_weight[0],
        key_matrix[0],
        value_matrix[0],
        o_weight[0],
        gate_weight[0],
        up_weight[0],
        down_weight[0],
    )
    section = lax.axis_index("section")
    first = section == 0
    micro = doc_lengths.shape[0]
    rows = block_input.shape[0] // micro
    width = block_input.shape[1]
    inputs = block_input.reshape(micro, rows, width)
    cotangents = out_cotangent.reshape(micro, rows, width)
    offsets, allowed_all = doc_tables(doc_lengths, rows)
    cosine_all, sine_all = rope_tables(offsets, HEAD_SIZE)
    outputs = jnp.zeros((micro, rows, width), jnp.float32)
    arrived = jnp.zeros((rows, width), jnp.bfloat16)
    kept_ticks = []
    for tick in range(micro + 1):
        slot = tick - section
        valid = (slot >= 0) & (slot < micro)
        place = jnp.clip(slot, 0, micro - 1)
        hidden = jnp.where(first, pick(inputs, place), arrived).astype(jnp.float32)
        result, kept = layer_forward(
            hidden,
            pick(cosine_all, place),
            pick(sine_all, place),
            pick(allowed_all, place),
            weights,
        )
        kept_ticks.append(kept)
        outputs = lax.dynamic_update_index_in_dim(
            outputs, jnp.where(valid, result, pick(outputs, place)), place, 0
        )
        if tick < micro:
            arrived = passed_along(result.astype(jnp.bfloat16), "section", 1)

    def choose(early, late):
        return jnp.where(first, early, late)

    grads_in = jnp.zeros((micro, rows, width), jnp.float32)
    returned = jnp.zeros((rows, width), jnp.bfloat16)
    attn_totals = (
        jnp.zeros(weights[4].shape, jnp.float32),
        jnp.zeros(weights[5].shape, jnp.float32),
        jnp.zeros(weights[6].shape, jnp.float32),
        jnp.zeros(weights[7].shape, jnp.float32),
    )
    mlp_totals = (
        jnp.zeros(weights[8].shape, jnp.float32),
        jnp.zeros(weights[9].shape, jnp.float32),
        jnp.zeros(weights[10].shape, jnp.float32),
    )
    gain_totals = (
        jnp.zeros(weights[0].shape, jnp.float32),
        jnp.zeros(weights[1].shape, jnp.float32),
        jnp.zeros(weights[2].shape, jnp.float32),
        jnp.zeros(weights[3].shape, jnp.float32),
    )
    for tick in range(micro + 1):
        slot = tick - 1 + section
        valid = (slot >= 0) & (slot < micro)
        place = jnp.clip(slot, 0, micro - 1)
        grad_out = jnp.where(first, returned, pick(cotangents, place)).astype(jnp.float32)
        grad_out = jnp.where(valid, grad_out, 0.0)
        kept = jax.tree.map(choose, kept_ticks[max(tick - 1, 0)], kept_ticks[min(tick + 1, micro)])
        middle_grad, mlp_part, mlp_terms = mlp_backward(grad_out, kept, weights)
        mlp_totals = tuple((total + term for total, term in zip(mlp_totals, mlp_terms)))
        grad_in, attn_parts, attn_terms = attention_backward(
            middle_grad,
            kept,
            pick(cosine_all, place),
            pick(sine_all, place),
            pick(allowed_all, place),
            weights,
        )
        attn_totals = tuple((total + term for total, term in zip(attn_totals, attn_terms)))
        gain_totals = (
            gain_totals[0] + attn_parts[0],
            gain_totals[1] + attn_parts[1],
            gain_totals[2] + attn_parts[2],
            gain_totals[3] + mlp_part,
        )
        grads_in = lax.dynamic_update_index_in_dim(
            grads_in, jnp.where(valid, grad_in, pick(grads_in, place)), place, 0
        )
        if tick < micro:
            returned = passed_along(grad_in.astype(jnp.bfloat16), "section", -1)
    summed = (
        lax.psum_scatter(
            attn_totals[0].astype(jnp.bfloat16), "dp", scatter_dimension=0, tiled=True
        ).astype(jnp.float32),
        lax.psum_scatter(
            attn_totals[1].astype(jnp.bfloat16), "dp", scatter_dimension=0, tiled=True
        ).astype(jnp.float32),
        lax.psum_scatter(
            attn_totals[2].astype(jnp.bfloat16), "dp", scatter_dimension=0, tiled=True
        ).astype(jnp.float32),
        lax.psum_scatter(
            attn_totals[3].astype(jnp.bfloat16), "dp", scatter_dimension=0, tiled=True
        ).astype(jnp.float32),
        lax.psum_scatter(
            mlp_totals[0].astype(jnp.bfloat16), "dp", scatter_dimension=0, tiled=True
        ).astype(jnp.float32),
        lax.psum_scatter(
            mlp_totals[1].astype(jnp.bfloat16), "dp", scatter_dimension=0, tiled=True
        ).astype(jnp.float32),
        lax.psum_scatter(
            mlp_totals[2].astype(jnp.bfloat16), "dp", scatter_dimension=0, tiled=True
        ).astype(jnp.float32),
    )
    attn_done = summed[:4]
    mlp_done = summed[4:]
    gains = lax.psum(
        (gain_totals[0], gain_totals[1], gain_totals[2], gain_totals[3]), ("dp", "tensor")
    )
    return (
        outputs.reshape(1, micro * rows, width),
        grads_in.reshape(1, micro * rows, width),
        gains[0][None],
        gains[1][None],
        gains[2][None],
        gains[3][None],
        attn_done[0][None],
        attn_done[1][None],
        attn_done[2][None],
        attn_done[3][None],
        mlp_done[0][None],
        mlp_done[1][None],
        mlp_done[2][None],
    )


def solution(mesh):
    return jax.shard_map(
        shards,
        mesh=mesh,
        in_specs=(
            P("dp", None),
            P("dp", None),
            P("dp", None),
            P("section", None),
            P("section", None),
            P("section", None),
            P("section", None),
            P("section", None, "tensor"),
            P("section", None, "tensor"),
            P("section", None, "tensor"),
            P("section", None, "tensor"),
            P("section", None, "tensor"),
            P("section", None, "tensor"),
            P("section", None, "tensor"),
        ),
        out_specs=(
            P("section", "dp", None),
            P("section", "dp", None),
            P("section", None),
            P("section", None),
            P("section", None),
            P("section", None),
            P("section", "dp", "tensor"),
            P("section", "dp", "tensor"),
            P("section", "dp", "tensor"),
            P("section", "dp", "tensor"),
            P("section", "dp", "tensor"),
            P("section", "dp", "tensor"),
            P("section", "dp", "tensor"),
        ),
        check_vma=False,
    )
```

profile of v0, /device:TPU:0, one launch (start us, length us, event | category | flops | bytes accessed | tf_op | source)
XLA Modules:
  0.0 1928.8 jit_solution(11080096997020907001)
XLA Ops:
  7.9 4.2 copy.175
  39.2 27.7 %all-reduce.14.cloned.1.call-done = f32[256,1024]{1,0:T(8,128)} async-done(((f32[256,1024]{1,0:T(8,128)}), f32[256,1024]{1,0:T(8,128)}) %all-reduce.14.cloned.1.call-update) | async-done | bytes 1048592 | tf_op jit(solution)/shard_map/psum | solution.py:133
  77.1 26.6 %all-reduce.16.cloned.1.call-done = f32[256,1024]{1,0:T(8,128)} async-done(((f32[256,1024]{1,0:T(8,128)}), f32[256,1024]{1,0:T(8,128)}) %all-reduce.16.cloned.1.call-update) | async-done | bytes 1048592 | tf_op jit(solution)/shard_map/psum | solution.py:143
  105.5 3.8 collective-permute-start
  109.3 11.4 collective-permute-done
  136.2 27.2 %all-reduce.18.cloned.1.call-done = f32[256,1024]{1,0:T(8,128)} async-done(((f32[256,1024]{1,0:T(8,128)}), f32[256,1024]{1,0:T(8,128)}) %all-reduce.18.cloned.1.call-update) | async-done | bytes 1048592 | tf_op jit(solution)/shard_map/psum | solution.py:133
  180.9 26.5 %all-reduce.30.cloned.1.call-done = (f32[256,1024]{1,0:T(8,128)}, f32[256,1024]{1,0:T(8,128)}) async-done(((f32[256,1024]{1,0:T(8,128)}, f32[256,1024]{1,0:T(8,128)}), (f32[256,1024]{1,0:T(8,128)}, f32[256,1024]{1,0:T(8,128)})) %all-reduce.30.cloned.1.call-update) | async-done | bytes 2097168 | tf_op jit(solution)/shard_map/psum | solution.py:143
  207.4 4.3 multiply_reduce_fusion.2
  211.8 4.5 collective-permute-start.1
  254.1 28.8 %all-reduce.28.cloned.1.call-done = (f32[256,1024]{1,0:T(8,128)}, f32[256,1024]{1,0:T(8,128)}) async-done(((f32[256,1024]{1,0:T(8,128)}, f32[256,1024]{1,0:T(8,128)}), (f32[256,1024]{1,0:T(8,128)}, f32[256,1024]{1,0:T(8,128)})) %all-reduce.28.cloned.1.call-update) | async-done | bytes 2097168 | tf_op jit(solution)/shard_map/psum | solution.py:133
  282.9 2.9 multiply_reduce_fusion.8
  294.2 12.6 collective-permute-done.2
  311.7 26.6 %all-reduce.20.cloned.1.call-done = f32[256,1024]{1,0:T(8,128)} async-done(((f32[256,1024]{1,0:T(8,128)}), f32[256,1024]{1,0:T(8,128)}) %all-reduce.20.cloned.1.call-update) | async-done | bytes 1048592 | tf_op jit(solution)/shard_map/psum | solution.py:191
  338.4 3.4 multiply_reduce_fusion.1
  364.1 24.3 %all-reduce.22.cloned.1.call-done = f32[256,1024]{1,0:T(8,128)} async-done(((f32[256,1024]{1,0:T(8,128)}), f32[256,1024]{1,0:T(8,128)}) %all-reduce.22.cloned.1.call-update) | async-done | bytes 1048592 | tf_op jit(solution)/shard_map/psum | solution.py:280
  388.5 3.0 multiply_reduce_fusion.7
  391.5 3.1 bitcast_dynamic-update-slice_fusion.1
  395.9 15.0 collective-permute-done.3
  412.2 5.6 multiply_convert_fusion.1
  423.5 3.1 fusion.6
  426.6 22.5 %all-reduce.24.cloned.1.call-done = f32[256,1024]{1,0:T(8,128)} async-done(((f32[256,1024]{1,0:T(8,128)}), f32[256,1024]{1,0:T(8,128)}) %all-reduce.24.cloned.1.call-update) | async-done | bytes 1048592 | tf_op jit(solution)/shard_map/psum | solution.py:191
  449.1 2.8 multiply_reduce_fusion
  495.0 2.8 add_convert_fusion.2
  501.3 2.8 add_convert_fusion.1
  519.9 175.7 %all-reduce = (f32[1,1024]{1,0:T(1,128)}, f32[1,128]{1,0:T(1,128)}, f32[1,128]{1,0:T(1,128)}, f32[1,1024]{1,0:T(1,128)}) all-reduce(f32[1,1024]{1,0:T(1,128)S(1)} %bitcast.757, f32[1,128]{1,0:T(1,128)S(1)} %add_bitcast_fusion.1, f32[1,128]{1,0:T(1,128)S(1)} %add_bitcast_fusion, ...), channel_id=1, replica_groups=mesh['section'=2,'dp'=32,'tensor'=2] {'dp','tensor'}, use_global_device_ids=true, to_apply=%region_51.52 | all-reduce | flops 2304 | bytes 18432 | tf_op jit(solution)/shard_map/psum | solution.py:421
  697.0 174.9 %reduce-scatter.12.cloned.1.call-done = bf16[32,512]{1,0:T(8,128)(2,1)} async-done(((bf16[1024,512]{1,0:T(8,128)(2,1)}), bf16[32,512]{1,0:T(8,128)(2,1)}) %reduce-scatter.12.cloned.1.call-update) | async-done | bytes 32784 | tf_op jit(solution)/shard_map/reduce_scatter | solution.py:403
  873.4 5.0 bitcast_dynamic-update-slice_fusion
  878.4 177.7 %reduce-scatter.8.cloned.1.call-done = bf16[32,1024]{1,0:T(8,128)(2,1)} async-done(((bf16[1024,1024]{1,0:T(8,128)(2,1)}), bf16[32,1024]{1,0:T(8,128)(2,1)}) %reduce-scatter.8.cloned.1.call-update) | async-done | bytes 65552 | tf_op jit(solution)/shard_map/reduce_scatter | solution.py:397
  1057.6 182.6 %reduce-scatter.14.cloned.1.call-done = bf16[32,1024]{1,0:T(8,128)(2,1)} async-done(((bf16[1024,1024]{1,0:T(8,128)(2,1)}), bf16[32,1024]{1,0:T(8,128)(2,1)}) %reduce-scatter.14.cloned.1.call-update) | async-done | bytes 65552 | tf_op jit(solution)/shard_map/reduce_scatter | solution.py:406
  1241.7 223.8 %reduce-scatter.16.cloned.1.call-done = bf16[32,1536]{1,0:T(8,128)(2,1)} async-done(((bf16[1024,1536]{1,0:T(8,128)(2,1)}), bf16[32,1536]{1,0:T(8,128)(2,1)}) %reduce-scatter.16.cloned.1.call-update) | async-done | bytes 98320 | tf_op jit(solution)/shard_map/reduce_scatter | solution.py:409
  1467.1 225.9 %reduce-scatter.18.cloned.1.call-done = bf16[32,1536]{1,0:T(8,128)(2,1)} async-done(((bf16[1024,1536]{1,0:T(8,128)(2,1)}), bf16[32,1536]{1,0:T(8,128)(2,1)}) %reduce-scatter.18.cloned.1.call-update) | async-done | bytes 98320 | tf_op jit(solution)/shard_map/reduce_scatter | solution.py:412
  1694.6 225.9 %reduce-scatter.20.cloned.1.call-done = bf16[32,1536]{1,0:T(8,128)(2,1)} async-done(((bf16[1024,1536]{1,0:T(8,128)(2,1)}), bf16[32,1536]{1,0:T(8,128)(2,1)}) %reduce-scatter.20.cloned.1.call-update) | async-done | bytes 98320 | tf_op jit(solution)/shard_map/reduce_scatter | solution.py:415
  (789 shorter events, 224.4 us)
Async XLA Ops:
  7.2 67.8 %copy-start = (bf16[1,1024,1536]{2,1,0:T(8,128)(2,1)S(1)}, bf16[1,1024,1536]{2,1,0:T(8,128)(2,1)}, u32[]{:S(2)}) copy-start(bf16[1,1024,1536]{2,1,0:T(8,128)(2,1)} %param.27) | copy-start | bytes 9437188
  7.2 59.7 %all-reduce.14.cloned.1.call-start = ((), (), s32[]{:S(2)}) async-start(), calls=%async_computation.7 | async-start | bytes 2097152 | tf_op jit(solution)/shard_map/psum | solution.py:133
  39.1 30.5 %copy-start.186 = (f32[1,1024]{1,0:T(1,128)S(1)}, f32[1,1024]{1,0:T(1,128)}, u32[]{:S(2)}) copy-start(f32[1,1024]{1,0:T(1,128)} %param.20) | copy-start | bytes 12292
  39.1 64.6 %all-reduce.16.cloned.1.call-start = ((), (), s32[]{:S(2)}) async-start(), calls=%async_computation.8 | async-start | bytes 2097152 | tf_op jit(solution)/shard_map/psum | solution.py:143
  77.0 86.4 %all-reduce.18.cloned.1.call-start = ((), (), s32[]{:S(2)}) async-start(), calls=%async_computation.9 | async-start | bytes 2097152 | tf_op jit(solution)/shard_map/psum | solution.py:133
  103.7 17.1 copy-start.20
  103.7 17.9 copy-start.72
  105.5 16.5 copy-start.152
  105.5 15.2 collective-permute-start
  136.2 71.3 %all-reduce.30.cloned.1.call-start = ((), (), s32[]{:S(2)}) async-start(), calls=%async_computation.22 | async-start | bytes 4194304 | tf_op jit(solution)/shard_map/psum | solution.py:143
  179.1 103.8 %all-reduce.28.cloned.1.call-start = ((), (), s32[]{:S(2)}) async-start(), calls=%async_computation.21 | async-start | bytes 4194304 | tf_op jit(solution)/shard_map/psum | solution.py:133
  211.8 16.2 collective-permute-start.1
  252.4 30.5 %copy-start.257 = (f32[256]{0:T(256)S(1)}, f32[256]{0:T(256)}, u32[]{:S(2)}) copy-start(f32[256]{0:T(256)} %get-tuple-element.173) | copy-start | bytes 3076
  253.8 84.5 %all-reduce.20.cloned.1.call-start = ((), (), s32[]{:S(2)}) async-start(), calls=%async_computation.10 | async-start | bytes 2097152 | tf_op jit(solution)/shard_map/psum | solution.py:191
  290.6 16.3 collective-permute-start.2
  294.2 14.2 copy-start.166
  311.7 76.8 %all-reduce.22.cloned.1.call-start = ((), (), s32[]{:S(2)}) async-start(), calls=%async_computation.11 | async-start | bytes 2097152 | tf_op jit(solution)/shard_map/psum | solution.py:280
  361.8 26.7 %copy-start.248 = (f32[256]{0:T(256)S(1)}, f32[256]{0:T(256)}, u32[]{:S(2)}) copy-start(f32[256]{0:T(256)} %get-tuple-element.175) | copy-start | bytes 3076
  361.8 87.3 %all-reduce.24.cloned.1.call-start = ((), (), s32[]{:S(2)}) async-start(), calls=%async_computation.12 | async-start | bytes 2097152 | tf_op jit(solution)/shard_map/psum | solution.py:191
  364.1 27.3 %copy-start.261 = (f32[256]{0:T(256)S(1)}, f32[256]{0:T(256)}, u32[]{:S(2)}) copy-start(f32[256]{0:T(256)} %get-tuple-element.174) | copy-start | bytes 3076
  394.6 16.3 collective-permute-start.3
  422.4 95.9 %all-reduce.26.cloned.1.call-start = ((), (), s32[]{:S(2)}) async-start(), calls=%async_computation.20 | async-start | bytes 4194304 | tf_op jit(solution)/shard_map/psum | solution.py:143
  423.5 25.6 %copy-start.255 = (f32[256]{0:T(256)S(1)}, f32[256]{0:T(256)}, u32[]{:S(2)}) copy-start(f32[256]{0:T(256)} %get-tuple-element.64) | copy-start | bytes 3076
  471.8 223.9 %reduce-scatter.10.cloned.1.call-start = ((), (), s32[]{:S(2)}) async-start(), calls=%async_computation.14 | async-start | bytes 1081344 | tf_op jit(solution)/shard_map/reduce_scatter | solution.py:400
  475.7 396.3 %reduce-scatter.12.cloned.1.call-start = ((), (), s32[]{:S(2)}) async-start(), calls=%async_computation.15 | async-start | bytes 1081344 | tf_op jit(solution)/shard_map/reduce_scatter | solution.py:403
  479.3 576.8 %reduce-scatter.8.cloned.1.call-start = ((), (), s32[]{:S(2)}) async-start(), calls=%async_computation.13 | async-start | bytes 2162688 | tf_op jit(solution)/shard_map/reduce_scatter | solution.py:397
  483.8 756.5 %reduce-scatter.14.cloned.1.call-start = ((), (), s32[]{:S(2)}) async-start(), calls=%async_computation.16 | async-start | bytes 2162688 | tf_op jit(solution)/shard_map/reduce_scatter | solution.py:406
  490.5 975.1 %reduce-scatter.16.cloned.1.call-start = ((), (), s32[]{:S(2)}) async-start(), calls=%async_computation.17 | async-start | bytes 3244032 | tf_op jit(solution)/shard_map/reduce_scatter | solution.py:409
  497.8 1195.2 %reduce-scatter.18.cloned.1.call-start = ((), (), s32[]{:S(2)}) async-start(), calls=%async_computation.18 | async-start | bytes 3244032 | tf_op jit(solution)/shard_map/reduce_scatter | solution.py:412
  504.1 1416.3 %reduce-scatter.20.cloned.1.call-start = ((), (), s32[]{:S(2)}) async-start(), calls=%async_computation.19 | async-start | bytes 3244032 | tf_op jit(solution)/shard_map/reduce_scatter | solution.py:415
  518.1 355.3 %copy-start.260 = (f32[256]{0:T(256)S(1)}, f32[256]{0:T(256)}, u32[]{:S(2)}) copy-start(f32[256]{0:T(256)} %get-tuple-element.49) | copy-start | bytes 3076
  873.4 1048.7 %copy-start.1 = (bf16[1,1024,1536]{2,1,0:T(8,128)(2,1)S(1)}, bf16[1,1024,1536]{2,1,0:T(8,128)(2,1)}, u32[]{:S(2)}) copy-start(bf16[1,1024,1536]{2,1,0:T(8,128)(2,1)} %param.27) | copy-start | bytes 9437188
  (261 other events, 620.9 us)
Sparse Core Ops, SparseCore 0:
  39.2 27.6 all-reduce.13
  77.1 26.4 all-reduce.15
  136.3 27.1 all-reduce.17
  179.2 28.1 all-reduce.29
  254.0 28.8 all-reduce.27
  311.8 26.5 all-reduce.19
  361.9 26.5 all-reduce.21
  422.5 26.5 all-reduce.23
  471.9 28.1 all-reduce.25
  502.4 186.8 reduce-scatter.9
  691.7 180.2 reduce-scatter.11
  874.3 181.7 reduce-scatter.7
  1058.5 181.6 reduce-scatter.13
  1245.8 219.7 reduce-scatter.15
  1471.1 221.8 reduce-scatter.17
  1698.5 221.8 reduce-scatter.19
where the time goes:
time: 1940 us; the launch traced here: 1930 us
  waiting for transfers between devices  1460 us (75%)
  blocking collectives  176 us (9%)
  matrix products  114 us (6%)
  other arithmetic  79.8 us (4%)
  local copies, waits for them, and re-layouts  68.5 us (4%)
    reduce_scatter x1, waiting for transfers between devices, shards(): lax.psum_scatter(mlp_totals[2].astype(jnp.bfloat16), 'dp', scatter_dimens...  226 us
    reduce_scatter x1, waiting for transfers between devices, shards(): lax.psum_scatter(mlp_totals[1].astype(jnp.bfloat16), 'dp', scatter_dimens...  226 us
    reduce_scatter x1, waiting for transfers between devices, shards(): lax.psum_scatter(mlp_totals[0].astype(jnp.bfloat16), 'dp', scatter_dimens...  224 us
    reduce_scatter x1, waiting for transfers between devices, shards(): lax.psum_scatter(attn_totals[3].astype(jnp.bfloat16), 'dp', scatter_dimen...  183 us
    reduce_scatter x1, waiting for transfers between devices, shards(): lax.psum_scatter(attn_totals[0].astype(jnp.bfloat16), 'dp', scatter_dimen...  178 us
    psum x1, blocking collectives, shards(): lax.psum((gain_totals[0], gain_totals[1], gain_totals[2], gain_totals[3])...  176 us
    reduce_scatter x1, waiting for transfers between devices, shards(): lax.psum_scatter(attn_totals[2].astype(jnp.bfloat16), 'dp', scatter_dimen...  175 us
    psum x3, waiting for transfers between devices, layer_forward(): lax.psum(lax.dot_general(mixed, o_weight, CONTRACT_COLS, preferred_elemen...  83.7 us
  transfers between devices with their start and end apart: 20, of which 17 were waited for; matrix products, arithmetic and copies ran while one was open for 4% of the time, Pallas kernels for 0%

commit v1 on v0

v1 whole, which is shorter than its diff:
```python
import functools

import jax
import jax.numpy as jnp
import numpy as np
from jax import lax
from jax.experimental import pallas as pl
from jax.experimental.pallas import tpu as pltpu
from jax.sharding import PartitionSpec as P

EPSILON = 1e-06
THETA = 1000000.0
HEAD = 128
ROW = 256
WIDTH = 1024
BLOCK = 32
SCORE_SCALE = HEAD ** (-0.5)
MESH = pl.DeviceIdType.MESH
BF16, F32 = jnp.bfloat16, jnp.float32
NT = (((1,), (1,)), ((), ()))
TN = (((0,), (0,)), ((), ()))

CHUNK = 512
GATE, UP, DOWN, QUERY, KEY, VALUE, OUT = 0, 3, 6, 9, 11, 12, 13
CHUNKS = 15
MLP_CHUNKS = 9
ORDERS = (("z", "y", "x"), ("y", "z", "x"))
COUNTS = (8, 7)
LAGS = (0, 0, 2, 2, 4, 6, 6, 8)
GAIN_ROWS = 24


def remote(src, dst, send_sem, recv_sem, device):
    return pltpu.make_async_remote_copy(
        src_ref=src,
        dst_ref=dst,
        send_sem=send_sem,
        recv_sem=recv_sem,
        device_id=device,
        device_id_type=MESH,
    )


def dot(left, right, form=None):
    if form is None:
        return jnp.dot(left, right, preferred_element_type=F32)
    return lax.dot_general(left, right, form, preferred_element_type=F32)


class Place:
    def __init__(self):
        dp = lax.axis_index("dp")
        self.at = {"z": dp // 8, "x": dp // 4 % 2, "y": dp % 4}

    def device(self, axis, index):
        at = {**self.at, axis: index}
        return {"dp": at["z"] * 8 + at["x"] * 4 + at["y"]}


def ring_phases(order):
    found, done = [], []
    for axis in order:
        left = [name for name in ("z", "x", "y") if name not in done and name != axis]
        halved = None if axis == "x" else "x" if "x" in left else left[0]
        shape = []
        for name in left:
            size = 2 if name == "x" else 4
            shape.append(size // 2 if name == halved else size)
        found.append((axis, tuple(done), halved, (*shape, 32, CHUNK)))
        done.append(axis)
    return found


def ring_scratch(order, count):
    found = []
    for _, _, halved, shape in ring_phases(order):
        parts = 6 if halved else 1
        found.append(pltpu.VMEM((count, parts, *shape), BF16))
        found.append(pltpu.SemaphoreType.DMA((count, parts)))
        found.append(pltpu.SemaphoreType.DMA((count, parts)))
    return found


def ring_stages(order, grads, first, scratch, place, finish):
    stages = []
    for step, (axis, done, halved, _) in enumerate(ring_phases(order)):
        arrived, send_sem, recv_sem = scratch[3 * step : 3 * step + 3]
        mine = place.at[axis]

        def where(i, index, half, axis=axis, done=done, halved=halved):
            found = [2 * i + first]
            for name in ("z", "x", "y"):
                if name in done:
                    found.append(place.at[name])
                elif name == axis:
                    found.append(index)
                elif name == halved:
                    size = 1 if name == "x" else 2
                    found.append(pl.ds(half * size, size))
                else:
                    found.append(slice(None))
            return tuple(found)

        def put(i, half, total, step=step, mine=mine, where=where):
            if step == 2:
                finish(2 * i + first, total)
            else:
                grads[where(i, mine, half)] = total.astype(BF16)

        if halved is None:

            def swap(
                i, where=where, arrived=arrived, send_sem=send_sem, recv_sem=recv_sem, mine=mine, axis=axis
            ):
                return remote(
                    grads.at[where(i, 1 - mine, 0)],
                    arrived.at[i, 0],
                    send_sem.at[i, 0],
                    recv_sem.at[i, 0],
                    place.device(axis, 1 - mine),
                )

            def start(i, swap=swap):
                swap(i).start()

            def end(i, swap=swap, arrived=arrived, where=where, mine=mine, put=put):
                swap(i).wait()
                put(i, 0, grads[where(i, mine, 0)].astype(F32) + arrived[i, 0].astype(F32))

            stages += [start, end]
            continue

        right, left = lax.rem(mine + 1, 4), lax.rem(mine + 3, 4)
        across = lax.rem(mine + 2, 4)
        sends = (
            (across, 0, right),
            (across, 1, left),
            (right, 1, right),
            (left, 0, left),
            (right, 0, right),
            (left, 1, left),
        )

        def send(
            i, k, where=where, arrived=arrived, send_sem=send_sem, recv_sem=recv_sem, axis=axis, sends=sends
        ):
            index, half, to = sends[k]
            return remote(
                grads.at[where(i, index, half)],
                arrived.at[i, k],
                send_sem.at[i, k],
                recv_sem.at[i, k],
                place.device(axis, to),
            )

        def start(i, send=send):
            for k in range(4):
                send(i, k).start()

        def pass_on(i, send=send, arrived=arrived, where=where, sends=sends):
            for k in (0, 1):
                send(i, k).wait_recv()
                index, half, _ = sends[4 + k]
                at = where(i, index, half)
                grads[at] = (grads[at].astype(F32) + arrived[i, k].astype(F32)).astype(BF16)
                send(i, 4 + k).start()

        def end(i, send=send, arrived=arrived, where=where, mine=mine, put=put):
            for k in range(2, 6):
                send(i, k).wait_recv()
            for k in range(6):
                send(i, k).wait_send()
            for half in (0, 1):
                own = grads[where(i, mine, half)].astype(F32)
                near = arrived[i, 4 - 2 * half].astype(F32)
                far = arrived[i, 3 + 2 * half].astype(F32)
                put(i, half, own + near + far)

        stages += [start, pass_on, end]
    return stages


def gain_scratch():
    found = [pltpu.VMEM((4, GAIN_ROWS, 128), F32)]
    for size in (4, 4, 2, 2):
        found.append(pltpu.SemaphoreType.DMA((size,)))
        found.append(pltpu.SemaphoreType.DMA((size,)))
        found.append(pltpu.VMEM((size, GAIN_ROWS, 128), F32))
    return found


def gain_axes(place):
    return (
        (4, place.at["y"], lambda k: place.device("y", k)),
        (4, place.at["z"], lambda k: place.device("z", k)),
        (2, place.at["x"], lambda k: place.device("x", k)),
        (2, lax.axis_index("tensor"), lambda k: {"tensor": k}),
    )


def gain_stages(total_ref, scratch, place):
    held = scratch[0]
    stages = []
    for step, (size, mine, device) in enumerate(gain_axes(place)):
        send_sem, recv_sem, slots = scratch[1 + 3 * step : 4 + 3 * step]
        src = held.at[step]
        dst = total_ref if step == 3 else held.at[step + 1]

        def send(k, src=src, slots=slots, send_sem=send_sem, recv_sem=recv_sem, size=size, mine=mine, device=device):
            to = lax.rem(mine + k, size)
            return remote(src, slots.at[mine], send_sem.at[k], recv_sem.at[mine], device(to))

        def arrival(k, src=src, slots=slots, send_sem=send_sem, recv_sem=recv_sem, size=size, mine=mine, device=device):
            frm = lax.rem(mine + k, size)
            return remote(src, slots.at[frm], send_sem.at[k], recv_sem.at[frm], device(frm))

        def start(i, send=send, src=src, slots=slots, size=size, mine=mine):
            slots[mine] = src[...]
            for k in range(1, size):
                send(k).start()

        def end(i, send=send, arrival=arrival, slots=slots, size=size, dst=dst):
            for k in range(1, size):
                arrival(k).wait_recv()
                send(k).wait_send()
            total = slots[0]
            for k in range(1, size):
                total = total + slots[k]
            dst[...] = total

        stages += [start, end]
    return stages


SCRATCH = dict(
    weights=pltpu.VMEM((CHUNKS, 4, 2, 4, 32, CHUNK), BF16),
    hidden=pltpu.VMEM((2 * ROW, WIDTH), BF16),
    normed=pltpu.VMEM((2 * ROW, WIDTH), BF16),
    heads=pltpu.VMEM((2 * ROW, 3072), BF16),
    query_rot=pltpu.VMEM((2 * ROW, 1024), BF16),
    key_rot=pltpu.VMEM((2 * ROW, 512), BF16),
    probs=pltpu.VMEM((2, 8, ROW, ROW), BF16),
    middle=pltpu.VMEM((2 * ROW, WIDTH), F32),
    normed_two=pltpu.VMEM((2 * ROW, WIDTH), BF16),
    ff=pltpu.VMEM((3, 2 * ROW, 1536), BF16),
    grad=pltpu.VMEM((2 * ROW, WIDTH), BF16),
    attended_grad=pltpu.VMEM((2 * ROW, WIDTH), BF16),
    mixed_grad=pltpu.VMEM((ROW, 1024), BF16),
    turned=pltpu.VMEM((2, WIDTH, 2 * ROW), BF16),
    mine=pltpu.VMEM((2, 4, ROW, 256), BF16),
    theirs=pltpu.VMEM((2, 4, ROW, 256), BF16),
    leaving=pltpu.VMEM((2 * ROW, WIDTH), BF16),
    stage=pltpu.VMEM((2 * ROW, WIDTH), F32),
    cosine=pltpu.VMEM((2 * ROW, HEAD), F32),
    sine=pltpu.VMEM((2 * ROW, HEAD), F32),
    bias=pltpu.VMEM((2 * ROW, ROW), F32),
    scale_one=pltpu.VMEM((2 * ROW, 128), F32),
    scale_two=pltpu.VMEM((2 * ROW, 128), F32),
    wide=pltpu.VMEM((2, ROW, CHUNK), F32),
    weight_sem=pltpu.SemaphoreType.DMA((CHUNKS,)),
    input_sem=pltpu.SemaphoreType.DMA((2,)),
    output_sem=pltpu.SemaphoreType.DMA((2, 2)),
    mine_sem=pltpu.SemaphoreType.DMA((2, 4)),
    theirs_sem=pltpu.SemaphoreType.DMA((2, 4)),
    cross_send=pltpu.SemaphoreType.DMA((2, 2)),
    cross_recv=pltpu.SemaphoreType.DMA((2, 2)),
    relay_send=pltpu.SemaphoreType.DMA((2, 2)),
    relay_recv=pltpu.SemaphoreType.DMA((2, 2)),
)


def rows_of(micro):
    return pl.ds(pl.multiple_of(micro * ROW, ROW), ROW)


def over_rows(micro, body):
    def one(block, carry):
        body(
            pl.ds(pl.multiple_of(micro * ROW + block * BLOCK, BLOCK), BLOCK),
            pl.ds(pl.multiple_of(block * BLOCK, BLOCK), BLOCK),
        )
        return carry

    lax.fori_loop(0, ROW // BLOCK, one, 0)


def columns(index, size=CHUNK):
    if isinstance(index, int):
        return pl.ds(index * size, size)
    return pl.ds(pl.multiple_of(index * size, size), size)


def inverse_rms(value):
    return lax.rsqrt(jnp.mean(value * value, axis=-1, keepdims=True) + EPSILON)


def kernel(
    lengths,
    block_input,
    cotangent,
    attn_gain,
    q_gain,
    k_gain,
    mlp_gain,
    q_weight,
    key_matrix,
    value_matrix,
    o_weight,
    gate_weight,
    up_weight,
    down_weight,
    table,
    hidden_out,
    hidden_grad,
    grads_out,
    gains_out,
    *scratch,
):
    s = dict(zip(SCRATCH, scratch))
    scratch = scratch[len(SCRATCH) :]
    weights, hidden, normed, heads = s["weights"], s["hidden"], s["normed"], s["heads"]
    query_rot, key_rot, probs = s["query_rot"], s["key_rot"], s["probs"]
    middle, normed_two, ff, grad = s["middle"], s["normed_two"], s["ff"], s["grad"]
    attended_grad, mixed_grad, turned = s["attended_grad"], s["mixed_grad"], s["turned"]
    mine, theirs, leaving, stage = s["mine"], s["theirs"], s["leaving"], s["stage"]
    cosine, sine, bias = s["cosine"], s["sine"], s["bias"]
    scale_one, scale_two, wide = s["scale_one"], s["scale_two"], s["wide"]
    place = Place()
    section, tensor = lax.axis_index("section"), lax.axis_index("tensor")
    over_tensor, over_section = {"tensor": 1 - tensor}, {"section": 1 - section}

    barrier = pltpu.get_barrier_semaphore()
    for size, own, device in gain_axes(place):
        for k in range(1, size):
            pl.semaphore_signal(
                barrier, inc=1, device_id=device(lax.rem(own + k, size)), device_id_type=MESH
            )
    pl.semaphore_signal(barrier, inc=1, device_id=over_section, device_id_type=MESH)

    sources = (
        [(q_weight, 0), (q_weight, 1), (key_matrix, 0), (value_matrix, 0), (o_weight, 0), (o_weight, 1)],
        [(ref, k) for ref in (gate_weight, up_weight, down_weight) for k in range(3)],
    )

    def load(chunk):
        ref, part = sources[1][chunk] if chunk < MLP_CHUNKS else sources[0][chunk - MLP_CHUNKS]
        return pltpu.make_async_copy(
            ref.at[:, :, :, :, columns(part)], weights.at[chunk], s["weight_sem"].at[chunk]
        )

    def load_input(micro):
        rows = rows_of(micro)
        return pltpu.make_async_copy(block_input.at[rows], hidden.at[rows], s["input_sem"].at[micro])

    def load_cotangent(micro):
        rows = rows_of(micro)
        return pltpu.make_async_copy(cotangent.at[rows], grad.at[rows], s["input_sem"].at[micro])

    @pl.when(section == 0)
    def _():
        load_input(0).start()
        load_input(1).start()

    for chunk in (9, 10, 11, 12, 13, 14, 0, 3, 1, 4, 2, 5, 6, 7, 8):
        load(chunk).start()

    @pl.when(section == 1)
    def _():
        load_cotangent(0).start()
        load_cotangent(1).start()

    gains = scratch[-13]
    gains[0] = jnp.zeros((GAIN_ROWS, 128), F32)

    def tables(micro, carry):
        rows = rows_of(micro)
        ends = [lengths[micro, 0]]
        for k in (1, 2):
            ends.append(ends[-1] + lengths[micro, k])

        def begins(shape):
            at = lax.broadcasted_iota(jnp.int32, shape, 0)
            found = jnp.zeros(shape, jnp.int32)
            for end in ends:
                found = jnp.where(at >= end, end, found)
            return at, found

        at, begin = begins((ROW, HEAD))
        chosen = (at - begin) == lax.broadcasted_iota(jnp.int32, (ROW, HEAD), 1)
        both = dot(chosen.astype(F32).astype(BF16), table[...])
        cosine[rows] = both[:, :128] + both[:, 128:256]
        sine[rows] = both[:, 256:384] + both[:, 384:]
        at, begin = begins((ROW, ROW))
        column = lax.broadcasted_iota(jnp.int32, (ROW, ROW), 1)
        bias[rows] = jnp.where((column >= begin) & (column <= at), 0.0, -1e9)
        return carry

    lax.fori_loop(0, 2, tables, 0)
    pl.semaphore_wait(barrier, 9)

    def pair(slot, part):
        return remote(
            mine.at[slot, part],
            theirs.at[slot, part],
            s["mine_sem"].at[slot, part],
            s["theirs_sem"].at[slot, part],
            over_tensor,
        )

    def pair_start(slot, part, value):
        mine[slot, part] = value.astype(BF16)
        pair(slot, part).start()

    def pair_wait(slot):
        for part in range(4):
            pair(slot, part).wait()

    def pair_sum(slot, block):
        return jnp.concatenate(
            [
                mine[slot, part, block].astype(F32) + theirs[slot, part, block].astype(F32)
                for part in range(4)
            ],
            axis=1,
        )

    def half_rows(micro):
        return pl.ds(pl.multiple_of(micro * ROW + tensor * (ROW // 2), ROW // 2), ROW // 2)

    def cross(way, micro):
        rows = half_rows(micro)
        into = hidden if way == 0 else grad
        return remote(
            leaving.at[rows],
            into.at[rows],
            s["cross_send"].at[way, micro],
            s["cross_recv"].at[way, micro],
            over_section,
        )

    def arrive(way, micro):
        rows = half_rows(micro)
        into = hidden if way == 0 else grad
        cross(way, micro).wait_recv()
        relay = remote(
            into.at[rows],
            into.at[rows],
            s["relay_send"].at[way, micro],
            s["relay_recv"].at[way, micro],
            over_tensor,
        )
        relay.start()
        relay.wait()

    def output(way, micro):
        rows = rows_of(micro)
        into = hidden_out if way == 0 else hidden_grad
        return pltpu.make_async_copy(stage.at[rows], into.at[rows], s["output_sem"].at[way, micro])

    def weight(chunk):
        return weights[chunk].reshape(WIDTH, CHUNK)

    def weight_part(chunk, part):
        return weights[chunk, part].reshape(256, CHUNK)

    def once(micro, chunks):
        @pl.when(micro == 0)
        def _():
            for chunk in chunks:
                load(chunk).wait()

    def rotated(value, cos, sin):
        return value * cos + pltpu.roll(value, HEAD // 2, 1) * sin

    def unrotated(value, cos, sin):
        return value * cos - pltpu.roll(value, HEAD // 2, 1) * sin

    def forward(micro, carry):
        rows = rows_of(micro)

        @pl.when(section == 0)
        def _():
            load_input(micro).wait()

        @pl.when(section == 1)
        def _():
            arrive(0, micro)

        def norm_one(at, block):
            value = hidden[at].astype(F32)
            scale = inverse_rms(value)
            normed[at] = (value * scale * attn_gain[...]).astype(BF16)
            scale_one[at] = jnp.broadcast_to(scale, (BLOCK, 128))

        over_rows(micro, norm_one)
        once(micro, range(QUERY, OUT))
        for chunk in range(4):
            wide[0] = dot(normed[rows], weight(QUERY + chunk))
            if chunk == 3:
                heads[rows, columns(chunk)] = wide[0].astype(BF16)
                continue
            gain = q_gain if chunk < 2 else k_gain
            for k in range(4):
                value = wide[0, :, columns(k, HEAD)]
                heads[rows, columns(chunk * 4 + k, HEAD)] = value.astype(BF16)
                turn = rotated(value * inverse_rms(value) * gain[...], cosine[rows], sine[rows])
                if chunk < 2:
                    query_rot[rows, columns(chunk * 4 + k, HEAD)] = turn.astype(BF16)
                else:
                    key_rot[rows, columns(k, HEAD)] = turn.astype(BF16)

        def attend(group, carry):
            keys = key_rot[rows, columns(group, HEAD)]
            values = heads[rows, columns(12 + group, HEAD)]
            for k in range(2):
                head = 2 * group + k
                scores = dot(query_rot[rows, columns(head, HEAD)], keys, NT) * SCORE_SCALE + bias[rows]
                peak = jnp.max(scores, axis=-1, keepdims=True)
                raw = jnp.exp(scores - peak)
                low = (raw / jnp.sum(raw, axis=-1, keepdims=True)).astype(BF16)
                probs[micro, head] = low
                heads[rows, columns(16 + head, HEAD)] = dot(low, values).astype(BF16)
            return carry

        lax.fori_loop(0, 4, attend, 0)
        once(micro, (OUT, OUT + 1))

        def attended(part, carry):
            value = dot(heads[rows, columns(4)], weight_part(OUT, part), NT)
            value = value + dot(heads[rows, columns(5)], weight_part(OUT + 1, part), NT)
            pair_start(0, part, value)
            return carry

        lax.fori_loop(0, 4, attended, 0)
        pair_wait(0)

        def norm_two(at, block):
            value = hidden[at].astype(F32) + pair_sum(0, block)
            middle[at] = value
            scale = inverse_rms(value)
            normed_two[at] = (value * scale * mlp_gain[...]).astype(BF16)
            scale_two[at] = jnp.broadcast_to(scale, (BLOCK, 128))

        over_rows(micro, norm_two)
        once(micro, range(QUERY))

        def hidden_units(chunk, carry):
            wide[0] = dot(normed_two[rows], weight(GATE + chunk))
            wide[1] = dot(normed_two[rows], weight(UP + chunk))

            def silu(at, block):
                gate, up = wide[0, block], wide[1, block]
                ff[0, at, columns(chunk)] = gate.astype(BF16)
                ff[1, at, columns(chunk)] = up.astype(BF16)
                ff[2, at, columns(chunk)] = (gate * jax.nn.sigmoid(gate) * up).astype(BF16)

            over_rows(micro, silu)
            return carry

        lax.fori_loop(0, 3, hidden_units, 0)

        def moved(part, carry):
            value = dot(ff[2, rows, columns(0)], weight_part(DOWN, part), NT)
            for k in (1, 2):
                value = value + dot(ff[2, rows, columns(k)], weight_part(DOWN + k, part), NT)
            pair_start(1, part, value)
            return carry

        lax.fori_loop(0, 4, moved, 0)
        pair_wait(1)

        def result(at, block):
            value = middle[at] + pair_sum(1, block)
            stage[at] = value
            leaving[at] = value.astype(BF16)

        over_rows(micro, result)
        output(0, micro).start()

        @pl.when(section == 0)
        def _():
            cross(0, micro).start()

        return carry

    lax.fori_loop(0, 2, forward, 0)

    def norm_back(total, value, scale, gain):
        inner = total * gain
        return scale * inner - value * (scale * scale * scale) * jnp.mean(
            inner * value, axis=-1, keepdims=True
        )

    def add_gain(row, value):
        gains[0, row : row + 1] = gains[0, row : row + 1] + value

    def add_gains(row, part, value):
        for k in range(2):
            at = pl.ds(row + part * 2 + k, 1)
            gains[0, at] = gains[0, at] + value[:, k * 128 : (k + 1) * 128]

    def turn(slot, value):
        for k in range(4):
            turned[slot, k * 256 : (k + 1) * 256] = value[:, columns(k, 256)].T

    def weight_grad(chunk, slot, right):
        for part in range(4):
            value = dot(turned[slot, columns(part, 256)], right)
            weights[chunk, part] = value.astype(BF16).reshape(2, 4, 32, CHUNK)

    def finish(chunk, total):
        if total.shape[0] == 1:
            total = total[0]
        grads_out[chunk] = total

    rings = []
    for first, (order, count) in enumerate(zip(ORDERS, COUNTS)):
        own, scratch = scratch[:9], scratch[9:]
        rings.append((count, LAGS, ring_stages(order, weights, first, own, place, finish)))

    def ring_start(chunk):
        for first in (0, 1):

            @pl.when(lax.rem(chunk, 2) == first)
            def _(first=first):
                rings[first][2][0]((chunk - first) // 2)

    def backward(micro, carry):
        rows = rows_of(micro)

        @pl.when(section == 0)
        def _():
            arrive(1, micro)
            cross(0, micro).wait_send()

        @pl.when(section == 1)
        def _():
            load_cotangent(micro).wait()

        def hidden_back(chunk, carry):
            wide[0] = dot(grad[rows], weight(DOWN + chunk))

            def silu_back(at, block):
                act_grad = wide[0, block]
                gate, up = ff[0, at, columns(chunk)].astype(F32), ff[1, at, columns(chunk)].astype(F32)
                sigma = jax.nn.sigmoid(gate)
                passed = act_grad * sigma
                ff[0, at, columns(chunk)] = (passed * up * (1.0 + gate * (1.0 - sigma))).astype(BF16)
                ff[1, at, columns(chunk)] = (passed * gate).astype(BF16)

            over_rows(micro, silu_back)
            return carry

        lax.fori_loop(0, 3, hidden_back, 0)

        def normed_two_back(part, carry):
            value = dot(ff[0, rows, columns(0)], weight_part(GATE, part), NT)
            for k in (1, 2):
                value = value + dot(ff[0, rows, columns(k)], weight_part(GATE + k, part), NT)
            for k in range(3):
                value = value + dot(ff[1, rows, columns(k)], weight_part(UP + k, part), NT)
            pair_start(0, part, value)
            scaled = middle[rows, columns(part, 256)] * scale_two[rows, :1]
            add_gains(8, part, jnp.sum(value * scaled, axis=0, keepdims=True))
            return carry

        lax.fori_loop(0, 4, normed_two_back, 0)
        pair_wait(0)
        output(0, micro).wait()

        def middle_back(at, block):
            value = grad[at].astype(F32) + norm_back(
                pair_sum(0, block), middle[at], scale_two[at, :1], mlp_gain[...]
            )
            stage[at] = value
            attended_grad[at] = value.astype(BF16)

        over_rows(micro, middle_back)

        @pl.when(micro == 1)
        def _():
            turn(0, normed_two)
            turn(1, grad)

            def one(chunk, carry):
                weight_grad(chunk, chunk // 6, ff[chunk // 3, :, columns(lax.rem(chunk, 3))])
                ring_start(chunk)
                return carry

            lax.fori_loop(0, MLP_CHUNKS, one, 0)

        for k in range(2):
            mixed_grad[:, columns(k)] = dot(attended_grad[rows], weight(OUT + k)).astype(BF16)

        def attend_back(group, carry):
            cos, sin = cosine[rows], sine[rows]
            keys = key_rot[rows, columns(group, HEAD)]
            values = heads[rows, columns(12 + group, HEAD)]
            key_rot_grad = jnp.zeros((ROW, HEAD), F32)
            value_grad = jnp.zeros((ROW, HEAD), F32)
            for k in range(2):
                head = 2 * group + k
                here = columns(head, HEAD)
                low = probs[micro, head]
                chance = low.astype(F32)
                out_grad = mixed_grad[:, here]
                weighted = chance * dot(out_grad, values, NT)
                score_grad = (weighted - chance * jnp.sum(weighted, axis=-1, keepdims=True)).astype(BF16)
                value_grad = value_grad + dot(low, out_grad, TN)
                key_rot_grad = key_rot_grad + dot(score_grad, query_rot[rows, here], TN)
                turn_grad = unrotated(dot(score_grad, keys) * SCORE_SCALE, cos, sin)
                query = heads[rows, here].astype(F32)
                scale = inverse_rms(query)
                add_gain(16, jnp.sum(turn_grad * query * scale, axis=0, keepdims=True))
                heads[rows, here] = norm_back(turn_grad, query, scale, q_gain[...]).astype(BF16)
            turn_grad = unrotated(key_rot_grad * SCORE_SCALE, cos, sin)
            here = columns(8 + group, HEAD)
            key = heads[rows, here].astype(F32)
            scale = inverse_rms(key)
            add_gain(17, jnp.sum(turn_grad * key * scale, axis=0, keepdims=True))
            heads[rows, here] = norm_back(turn_grad, key, scale, k_gain[...]).astype(BF16)
            heads[rows, columns(12 + group, HEAD)] = value_grad.astype(BF16)
            return carry

        lax.fori_loop(0, 4, attend_back, 0)

        def normed_back(part, carry):
            value = dot(heads[rows, columns(0)], weight_part(QUERY, part), NT)
            for k in (1, 2, 3):
                value = value + dot(heads[rows, columns(k)], weight_part(QUERY + k, part), NT)
            pair_start(1, part, value)
            scaled = hidden[rows, columns(part, 256)].astype(F32) * scale_one[rows, :1]
            add_gains(0, part, jnp.sum(value * scaled, axis=0, keepdims=True))
            return carry

        lax.fori_loop(0, 4, normed_back, 0)
        pair_wait(1)

        def hidden_back_end(at, block):
            value = stage[at] + norm_back(
                pair_sum(1, block), hidden[at].astype(F32), scale_one[at, :1], attn_gain[...]
            )
            stage[at] = value
            leaving[at] = value.astype(BF16)

        over_rows(micro, hidden_back_end)
        output(1, micro).start()

        @pl.when(section == 1)
        def _():
            cross(1, micro).start()

        return carry

    lax.fori_loop(0, 2, backward, 0)

    turn(0, normed)
    turn(1, attended_grad)

    def attention_grad(chunk, carry):
        weight_grad(MLP_CHUNKS + chunk, chunk // 4, heads[:, columns(chunk)])
        ring_start(MLP_CHUNKS + chunk)
        return carry

    lax.fori_loop(0, CHUNKS - MLP_CHUNKS, attention_grad, 0)

    groups = [(count, (None, *lags[1:]), stages) for count, lags, stages in rings]
    groups.append((1, (0, 2, 2, 4, 4, 6, 6, 8), gain_stages(gains_out, scratch, place)))

    def advance(now, carry):
        for step in range(8):
            for count, lags, stages in groups:
                if lags[step] is None:
                    continue
                i = now - lags[step]

                @pl.when((i >= 0) & (i < count))
                def _(i=i, run=stages[step]):
                    run(i)

        return carry

    lax.fori_loop(0, max(count + lags[-1] for count, lags, _ in groups), advance, 0)

    for micro in range(2):
        output(1, micro).wait()

        @pl.when(section == 1)
        def _(micro=micro):
            cross(1, micro).wait_send()


def rope_table():
    half = HEAD // 2
    rates = THETA ** (-2.0 * np.arange(half) / HEAD)
    angle = np.arange(HEAD)[:, None] * np.concatenate([rates, rates])[None]
    sign = np.where(np.arange(HEAD) < half, -1.0, 1.0)
    parts = []
    for value in (np.cos(angle), np.sin(angle) * sign):
        high = value.astype(jnp.bfloat16)
        parts += [high, (value - high.astype(np.float64)).astype(jnp.bfloat16)]
    return jnp.asarray(np.concatenate(parts, axis=1))


def by_place(weight):
    return weight.reshape(4, 2, 4, 32, weight.shape[-1])


def shards(
    block_input,
    doc_lengths,
    out_cotangent,
    attn_gain,
    q_gain,
    k_gain,
    mlp_gain,
    q_weight,
    key_matrix,
    value_matrix,
    o_weight,
    gate_weight,
    up_weight,
    down_weight,
):
    vmem = pl.BlockSpec(memory_space=pltpu.VMEM)
    smem = pl.BlockSpec(memory_space=pltpu.SMEM)
    anywhere = pl.BlockSpec(memory_space=pl.ANY)
    scratch = list(SCRATCH.values())
    for order, count in zip(ORDERS, COUNTS):
        scratch += ring_scratch(order, count)
    scratch += gain_scratch()
    full = jax.ShapeDtypeStruct(block_input.shape, F32)
    outputs, grads_in, grads, gains = pl.pallas_call(
        kernel,
        out_shape=(
            full,
            full,
            jax.ShapeDtypeStruct((CHUNKS, 32, CHUNK), F32),
            jax.ShapeDtypeStruct((GAIN_ROWS, 128), F32),
        ),
        in_specs=[smem, anywhere, anywhere] + [vmem] * 4 + [anywhere] * 7 + [vmem],
        out_specs=[anywhere, anywhere, vmem, vmem],
        scratch_shapes=scratch,
        compiler_params=pltpu.CompilerParams(
            collective_id=0, has_side_effects=True, vmem_limit_bytes=64 * 2**20 - 2**16
        ),
    )(
        doc_lengths,
        block_input,
        out_cotangent,
        attn_gain,
        q_gain,
        k_gain,
        mlp_gain,
        by_place(q_weight),
        by_place(key_matrix),
        by_place(value_matrix),
        by_place(o_weight),
        by_place(gate_weight),
        by_place(up_weight),
        by_place(down_weight),
        rope_table(),
    )

    def matrix(first, count):
        return jnp.concatenate([grads[first + k] for k in range(count)], axis=1)[None]

    flat = gains.reshape(1, -1)
    return (
        outputs[None],
        grads_in[None],
        flat[:, :1024],
        flat[:, 2048:2176],
        flat[:, 2176:2304],
        flat[:, 1024:2048],
        matrix(QUERY, 2),
        matrix(KEY, 1),
        matrix(VALUE, 1),
        matrix(OUT, 2),
        matrix(GATE, 3),
        matrix(UP, 3),
        matrix(DOWN, 3),
    )


def solution(mesh):
    weight = P("section", None, "tensor")
    gain = P("section", None)
    tokens = P("section", "dp", None)
    grad = P("section", "dp", "tensor")
    return jax.shard_map(
        shards,
        mesh=mesh,
        in_specs=(P("dp", None),) * 3 + (gain,) * 4 + (weight,) * 7,
        out_specs=(tokens,) * 2 + (gain,) * 4 + (grad,) * 7,
        check_vma=False,
    )
```

time: 1940 us -> 233 us (0.12)
  waiting for transfers between devices: 1460 us -> 0 us
  Pallas kernels: 0 us -> 223 us
  blocking collectives: 176 us -> 0 us
  matrix products: 114 us -> 0 us
  other arithmetic: 79.8 us -> 2.18 us
  local copies, waits for them, and re-layouts: 68.5 us -> 6.89 us
    reduce_scatter x7 -> x0, waiting for transfers between devices: 1210 us -> none  [the longest x1 226 us: shards(): lax.psum_scatter(mlp_totals[2].astype(jnp.bfloat16), 'dp', scatter_dimens...]
    pallas_call x0 -> x1, Pallas kernels: none -> 223 us  [shards(): pl.pallas_call(kernel, out_shape=(full, full, jax.ShapeDtypeStruct((CHUNK...]
    psum x9 -> x0, waiting for transfers between devices: 210 us -> none  [the longest x3 83.7 us: layer_forward(): lax.psum(lax.dot_general(mixed, o_weight, CONTRACT_COLS, preferred_elemen...]
    psum x1 -> x0, blocking collectives: 176 us -> none  [shards(): lax.psum((gain_totals[0], gain_totals[1], gain_totals[2], gain_totals[3])...]
    dot_general x84 -> x0, matrix products: 114 us -> none  [the longest x3 8.87 us: mlp_backward(): jnp.dot(moved_grad, down_weight, preferred_element_type=jnp.float32)]
    unnamed x546 -> x8, local copies, waits for them, and re-layouts: 44 us -> 3.67 us
    ppermute x4 -> x0, waiting for transfers between devices: 39.1 us -> none  [passed_along(): return lax.ppermute(shard, axis, pairs)]
    reduce_sum x22 -> x0, other arithmetic: 31.4 us -> none  [the longest x3 10.5 us: mlp_backward(): gain_part = jnp.sum(normed_part * middle * scale_two, axis=0)]
  transfers between devices with their start and end apart: 20 -> 0, of which waited for: 17 -> 0; matrix products, arithmetic and copies ran while one was open for 4% -> 0% of each run, Pallas kernels for 0% -> 0%
where the time goes in v1:
time: 233 us
  Pallas kernels  223 us (96%)
  local copies, waits for them, and re-layouts  6.89 us (3%)
    pallas_call x1, Pallas kernels, shards(): pl.pallas_call(kernel, out_shape=(full, full, jax.ShapeDtypeStruct((CHUNK...  223 us

profile of v1, /device:TPU:0, one launch (start us, length us, event | category | flops | bytes accessed | tf_op | source)
XLA Modules:
  0.0 233.1 jit_solution(15141691403749211167)
XLA Ops:
  0.7 223.4 %shard_map.246 = (f32[512,1024]{1,0:T(8,128)}, f32[512,1024]{1,0:T(8,128)}, f32[15,32,512]{2,1,0:T(8,128)}, f32[24,128]{1,0:T(8,128)}) custom-call(s32[2,4]{1,0:T(2,128)} %lengths.1, bf16[512,1024]{1,0:T(8,128)(2,1)} %block_input.1, bf16[512,1024]{1,0:T(8,128)(2,1)} %cotangent.1, f32[1,1024]{1,0:T(1,128)} %attn_gain.1, f32[1,128]{1,0:T(1,128)} %q_gain.1, ...), custom_call_target="tpu_custom_call" | custom-call | tf_op jit(solution)/shard_map/pallas_call | solution.py:833
  224.1 0.0 copy-start.2
  224.1 0.0 copy-start.1
  224.1 2.1 slice_bitcast_fusion.2
  226.2 0.8 maximum_bitcast_fusion
  226.9 0.7 maximum_bitcast_fusion.3
  227.7 0.7 maximum_bitcast_fusion.2
  228.3 0.0 copy-done.2
  228.4 0.6 fusion
  229.0 0.5 fusion.1
  229.5 0.0 copy-done.1
  229.5 0.0 copy-start
  229.5 1.3 copy.30
  230.8 1.0 copy-done
  231.8 1.3 copy.31
Async XLA Ops:
  224.1 4.3 %copy-start.2 = (f32[24,128]{1,0:T(8,128)S(1)}, f32[24,128]{1,0:T(8,128)}, u32[]{:S(2)}) copy-start(f32[24,128]{1,0:T(8,128)} %get-tuple-element.19) | copy-start | bytes 36868
  224.1 5.4 %copy-start.1 = (f32[512,1024]{1,0:T(8,128)S(1)}, f32[512,1024]{1,0:T(8,128)}, u32[]{:S(2)}) copy-start(f32[512,1024]{1,0:T(8,128)} %get-tuple-element.17) | copy-start | bytes 6291460
  229.5 2.3 %copy-start = (f32[512,1024]{1,0:T(8,128)S(1)}, f32[512,1024]{1,0:T(8,128)}, u32[]{:S(2)}) copy-start(f32[512,1024]{1,0:T(8,128)} %get-tuple-element.18) | copy-start | bytes 6291460

commit v2 on v1

--- a/solution.py
+++ b/solution.py
@@ -15,6 +15,7 @@
 WIDTH = 1024
 BLOCK = 32
 SCORE_SCALE = HEAD ** (-0.5)
+LOG2_E = 1.4426950408889634
 MESH = pl.DeviceIdType.MESH
 BF16, F32 = jnp.bfloat16, jnp.float32
 NT = (((1,), (1,)), ((), ()))
@@ -239,29 +240,33 @@
     heads=pltpu.VMEM((2 * ROW, 3072), BF16),
     query_rot=pltpu.VMEM((2 * ROW, 1024), BF16),
     key_rot=pltpu.VMEM((2 * ROW, 512), BF16),
-    probs=pltpu.VMEM((2, 8, ROW, ROW), BF16),
     middle=pltpu.VMEM((2 * ROW, WIDTH), F32),
     normed_two=pltpu.VMEM((2 * ROW, WIDTH), BF16),
     ff=pltpu.VMEM((3, 2 * ROW, 1536), BF16),
     grad=pltpu.VMEM((2 * ROW, WIDTH), BF16),
     attended_grad=pltpu.VMEM((2 * ROW, WIDTH), BF16),
     mixed_grad=pltpu.VMEM((ROW, 1024), BF16),
-    turned=pltpu.VMEM((2, WIDTH, 2 * ROW), BF16),
-    mine=pltpu.VMEM((2, 4, ROW, 256), BF16),
-    theirs=pltpu.VMEM((2, 4, ROW, 256), BF16),
+    turned=pltpu.VMEM((4, 4, 2, 4, 32, CHUNK), BF16),
+    mine=pltpu.VMEM((2, 2, ROW, CHUNK), BF16),
+    theirs=pltpu.VMEM((2, 2, ROW, CHUNK), BF16),
     leaving=pltpu.VMEM((2 * ROW, WIDTH), BF16),
     stage=pltpu.VMEM((2 * ROW, WIDTH), F32),
     cosine=pltpu.VMEM((2 * ROW, HEAD), F32),
     sine=pltpu.VMEM((2 * ROW, HEAD), F32),
     bias=pltpu.VMEM((2 * ROW, ROW), F32),
+    cosine_turned=pltpu.VMEM((2, HEAD, ROW), F32),
+    sine_turned=pltpu.VMEM((2, HEAD, ROW), F32),
+    bias_turned=pltpu.VMEM((2 * ROW, ROW), F32),
+    q_gain_turned=pltpu.VMEM((HEAD, HEAD), F32),
+    q_gain_sum=pltpu.VMEM((HEAD, ROW), F32),
     scale_one=pltpu.VMEM((2 * ROW, 128), F32),
     scale_two=pltpu.VMEM((2 * ROW, 128), F32),
     wide=pltpu.VMEM((2, ROW, CHUNK), F32),
     weight_sem=pltpu.SemaphoreType.DMA((CHUNKS,)),
     input_sem=pltpu.SemaphoreType.DMA((2,)),
     output_sem=pltpu.SemaphoreType.DMA((2, 2)),
-    mine_sem=pltpu.SemaphoreType.DMA((2, 4)),
-    theirs_sem=pltpu.SemaphoreType.DMA((2, 4)),
+    mine_sem=pltpu.SemaphoreType.DMA((2, 2)),
+    theirs_sem=pltpu.SemaphoreType.DMA((2, 2)),
     cross_send=pltpu.SemaphoreType.DMA((2, 2)),
     cross_recv=pltpu.SemaphoreType.DMA((2, 2)),
     relay_send=pltpu.SemaphoreType.DMA((2, 2)),
@@ -274,14 +279,11 @@
 
 
 def over_rows(micro, body):
-    def one(block, carry):
+    for block in range(ROW // BLOCK):
         body(
             pl.ds(pl.multiple_of(micro * ROW + block * BLOCK, BLOCK), BLOCK),
-            pl.ds(pl.multiple_of(block * BLOCK, BLOCK), BLOCK),
+            pl.ds(block * BLOCK, BLOCK),
         )
-        return carry
-
-    lax.fori_loop(0, ROW // BLOCK, one, 0)
 
 
 def columns(index, size=CHUNK):
@@ -319,7 +321,7 @@
     s = dict(zip(SCRATCH, scratch))
     scratch = scratch[len(SCRATCH) :]
     weights, hidden, normed, heads = s["weights"], s["hidden"], s["normed"], s["heads"]
-    query_rot, key_rot, probs = s["query_rot"], s["key_rot"], s["probs"]
+    query_rot, key_rot = s["query_rot"], s["key_rot"]
     middle, normed_two, ff, grad = s["middle"], s["normed_two"], s["ff"], s["grad"]
     attended_grad, mixed_grad, turned = s["attended_grad"], s["mixed_grad"], s["turned"]
     mine, theirs, leaving, stage = s["mine"], s["theirs"], s["leaving"], s["stage"]
@@ -378,8 +380,8 @@
         for k in (1, 2):
             ends.append(ends[-1] + lengths[micro, k])
 
-        def begins(shape):
-            at = lax.broadcasted_iota(jnp.int32, shape, 0)
+        def begins(shape, dim=0):
+            at = lax.broadcasted_iota(jnp.int32, shape, dim)
             found = jnp.zeros(shape, jnp.int32)
             for end in ends:
                 found = jnp.where(at >= end, end, found)
@@ -390,12 +392,18 @@
         both = dot(chosen.astype(F32).astype(BF16), table[...])
         cosine[rows] = both[:, :128] + both[:, 128:256]
         sine[rows] = both[:, 256:384] + both[:, 384:]
-        at, begin = begins((ROW, ROW))
-        column = lax.broadcasted_iota(jnp.int32, (ROW, ROW), 1)
-        bias[rows] = jnp.where((column >= begin) & (column <= at), 0.0, -1e9)
+        s["cosine_turned"][micro] = cosine[rows].T
+        s["sine_turned"][micro] = sine[rows].T
+        for dim, into in ((0, bias), (1, s["bias_turned"])):
+            at, begin = begins((ROW, ROW), dim)
+            key = lax.broadcasted_iota(jnp.int32, (ROW, ROW), 1 - dim)
+            into[rows] = jnp.where((key >= begin) & (key <= at), 0.0, -1e9)
         return carry
 
     lax.fori_loop(0, 2, tables, 0)
+    s["q_gain_turned"][...] = jnp.broadcast_to(q_gain[...], (HEAD, HEAD)).T
+    s["q_gain_sum"][...] = jnp.zeros((HEAD, ROW), F32)
+
     pl.semaphore_wait(barrier, 9)
 
     def pair(slot, part):
@@ -412,14 +420,14 @@
         pair(slot, part).start()
 
     def pair_wait(slot):
-        for part in range(4):
+        for part in range(2):
             pair(slot, part).wait()
 
     def pair_sum(slot, block):
         return jnp.concatenate(
             [
                 mine[slot, part, block].astype(F32) + theirs[slot, part, block].astype(F32)
-                for part in range(4)
+                for part in range(2)
             ],
             axis=1,
         )
@@ -460,8 +468,9 @@
     def weight(chunk):
         return weights[chunk].reshape(WIDTH, CHUNK)
 
-    def weight_part(chunk, part):
-        return weights[chunk, part].reshape(256, CHUNK)
+    def times_back(left, chunks, part):
+        right = [weights[chunk, 2 * part : 2 * part + 2].reshape(CHUNK, CHUNK) for chunk in chunks]
+        return dot(left, jnp.concatenate(right, axis=1), NT)
 
     def once(micro, chunks):
         @pl.when(micro == 0)
@@ -509,29 +518,30 @@
                 else:
                     key_rot[rows, columns(k, HEAD)] = turn.astype(BF16)
 
-        def attend(group, carry):
+        ones = jnp.ones((ROW, HEAD), BF16)
+
+        def attend(group):
             keys = key_rot[rows, columns(group, HEAD)]
             values = heads[rows, columns(12 + group, HEAD)]
             for k in range(2):
                 head = 2 * group + k
-                scores = dot(query_rot[rows, columns(head, HEAD)], keys, NT) * SCORE_SCALE + bias[rows]
-                peak = jnp.max(scores, axis=-1, keepdims=True)
-                raw = jnp.exp(scores - peak)
-                low = (raw / jnp.sum(raw, axis=-1, keepdims=True)).astype(BF16)
-                probs[micro, head] = low
-                heads[rows, columns(16 + head, HEAD)] = dot(low, values).astype(BF16)
-            return carry
-
-        lax.fori_loop(0, 4, attend, 0)
+                scores = dot(query_rot[rows, columns(head, HEAD)], keys, NT)
+                low = jnp.exp2(scores * (SCORE_SCALE * LOG2_E) + bias[rows]).astype(BF16)
+                both = dot(low, jnp.concatenate([values, ones], axis=1))
+                inverse = 1.0 / both[:, HEAD:]
+                heads[rows, columns(16 + head, HEAD)] = (both[:, :HEAD] * inverse).astype(BF16)
+
+        for index in range(4):
+            attend(index)
         once(micro, (OUT, OUT + 1))
 
-        def attended(part, carry):
-            value = dot(heads[rows, columns(4)], weight_part(OUT, part), NT)
-            value = value + dot(heads[rows, columns(5)], weight_part(OUT + 1, part), NT)
+        def attended(part):
+            value = times_back(heads[rows, 2048:], (OUT, OUT + 1), part)
             pair_start(0, part, value)
-            return carry
-
-        lax.fori_loop(0, 4, attended, 0)
+
+        for index in range(2):
+            attended(index)
+
         pair_wait(0)
 
         def norm_two(at, block):
@@ -544,7 +554,7 @@
         over_rows(micro, norm_two)
         once(micro, range(QUERY))
 
-        def hidden_units(chunk, carry):
+        def hidden_units(chunk):
             wide[0] = dot(normed_two[rows], weight(GATE + chunk))
             wide[1] = dot(normed_two[rows], weight(UP + chunk))
 
@@ -555,18 +565,17 @@
                 ff[2, at, columns(chunk)] = (gate * jax.nn.sigmoid(gate) * up).astype(BF16)
 
             over_rows(micro, silu)
-            return carry
-
-        lax.fori_loop(0, 3, hidden_units, 0)
-
-        def moved(part, carry):
-            value = dot(ff[2, rows, columns(0)], weight_part(DOWN, part), NT)
-            for k in (1, 2):
-                value = value + dot(ff[2, rows, columns(k)], weight_part(DOWN + k, part), NT)
+
+        for index in range(3):
+            hidden_units(index)
+
+        def moved(part):
+            value = times_back(ff[2, rows], range(DOWN, QUERY), part)
             pair_start(1, part, value)
-            return carry
-
-        lax.fori_loop(0, 4, moved, 0)
+
+        for index in range(2):
+            moved(index)
+
         pair_wait(1)
 
         def result(at, block):
@@ -595,17 +604,21 @@
         gains[0, row : row + 1] = gains[0, row : row + 1] + value
 
     def add_gains(row, part, value):
-        for k in range(2):
-            at = pl.ds(row + part * 2 + k, 1)
+        for k in range(4):
+            at = slice(row + part * 4 + k, row + part * 4 + k + 1)
             gains[0, at] = gains[0, at] + value[:, k * 128 : (k + 1) * 128]
 
     def turn(slot, value):
         for k in range(4):
-            turned[slot, k * 256 : (k + 1) * 256] = value[:, columns(k, 256)].T
+            turned[slot, k] = value[:, columns(k, 256)].T.reshape(2, 4, 32, CHUNK)
+
+    @pl.when(section == 0)
+    def _():
+        turn(0, normed_two)
 
     def weight_grad(chunk, slot, right):
         for part in range(4):
-            value = dot(turned[slot, columns(part, 256)], right)
+            value = dot(turned[slot, part].reshape(256, CHUNK), right)
             weights[chunk, part] = value.astype(BF16).reshape(2, 4, 32, CHUNK)
 
     def finish(chunk, total):
@@ -637,7 +650,7 @@
         def _():
             load_cotangent(micro).wait()
 
-        def hidden_back(chunk, carry):
+        def hidden_back(chunk):
             wide[0] = dot(grad[rows], weight(DOWN + chunk))
 
             def silu_back(at, block):
@@ -649,22 +662,19 @@
                 ff[1, at, columns(chunk)] = (passed * gate).astype(BF16)
 
             over_rows(micro, silu_back)
-            return carry
-
-        lax.fori_loop(0, 3, hidden_back, 0)
-
-        def normed_two_back(part, carry):
-            value = dot(ff[0, rows, columns(0)], weight_part(GATE, part), NT)
-            for k in (1, 2):
-                value = value + dot(ff[0, rows, columns(k)], weight_part(GATE + k, part), NT)
-            for k in range(3):
-                value = value + dot(ff[1, rows, columns(k)], weight_part(UP + k, part), NT)
+
+        for index in range(3):
+            hidden_back(index)
+
+        def normed_two_back(part):
+            left = jnp.concatenate([ff[0, rows], ff[1, rows]], axis=1)
+            value = times_back(left, range(GATE, DOWN), part)
             pair_start(0, part, value)
-            scaled = middle[rows, columns(part, 256)] * scale_two[rows, :1]
+            scaled = middle[rows, columns(part)] * scale_two[rows, :1]
             add_gains(8, part, jnp.sum(value * scaled, axis=0, keepdims=True))
-            return carry
-
-        lax.fori_loop(0, 4, normed_two_back, 0)
+
+        for index in range(2):
+            normed_two_back(index)
         pair_wait(0)
         output(0, micro).wait()
 
@@ -679,40 +689,54 @@
 
         @pl.when(micro == 1)
         def _():
-            turn(0, normed_two)
-            turn(1, grad)
+            @pl.when(section == 1)
+            def _():
+                turn(0, normed_two)
 
             def one(chunk, carry):
                 weight_grad(chunk, chunk // 6, ff[chunk // 3, :, columns(lax.rem(chunk, 3))])
                 ring_start(chunk)
                 return carry
 
-            lax.fori_loop(0, MLP_CHUNKS, one, 0)
+            lax.fori_loop(0, DOWN, one, 0)
+            turn(1, grad)
+            lax.fori_loop(DOWN, MLP_CHUNKS, one, 0)
 
         for k in range(2):
             mixed_grad[:, columns(k)] = dot(attended_grad[rows], weight(OUT + k)).astype(BF16)
 
-        def attend_back(group, carry):
+        def attend_back(group):
             cos, sin = cosine[rows], sine[rows]
+            cos_turned, sin_turned = s["cosine_turned"][micro], s["sine_turned"][micro]
+            gain_turned = jnp.concatenate([s["q_gain_turned"][...]] * 2, axis=1)
             keys = key_rot[rows, columns(group, HEAD)]
+            keys_turned = keys.T
             values = heads[rows, columns(12 + group, HEAD)]
             key_rot_grad = jnp.zeros((ROW, HEAD), F32)
             value_grad = jnp.zeros((ROW, HEAD), F32)
             for k in range(2):
                 head = 2 * group + k
                 here = columns(head, HEAD)
-                low = probs[micro, head]
-                chance = low.astype(F32)
+                queries = query_rot[rows, here]
                 out_grad = mixed_grad[:, here]
-                weighted = chance * dot(out_grad, values, NT)
-                score_grad = (weighted - chance * jnp.sum(weighted, axis=-1, keepdims=True)).astype(BF16)
-                value_grad = value_grad + dot(low, out_grad, TN)
-                key_rot_grad = key_rot_grad + dot(score_grad, query_rot[rows, here], TN)
-                turn_grad = unrotated(dot(score_grad, keys) * SCORE_SCALE, cos, sin)
-                query = heads[rows, here].astype(F32)
-                scale = inverse_rms(query)
-                add_gain(16, jnp.sum(turn_grad * query * scale, axis=0, keepdims=True))
-                heads[rows, here] = norm_back(turn_grad, query, scale, q_gain[...]).astype(BF16)
+                scores = dot(keys, queries, NT)
+                raw = jnp.exp2(scores * (SCORE_SCALE * LOG2_E) + s["bias_turned"][rows])
+                chance = raw * (1.0 / jnp.sum(raw, axis=0, keepdims=True))
+                weighted = chance * dot(values, out_grad, NT)
+                across = jnp.sum(weighted, axis=0, keepdims=True)
+                score_grad = (weighted - chance * across).astype(BF16)
+                value_grad = value_grad + dot(chance.astype(BF16), out_grad)
+                key_rot_grad = key_rot_grad + dot(score_grad, queries)
+                passed = dot(keys_turned, score_grad) * SCORE_SCALE
+                swapped = jnp.concatenate([passed[HEAD // 2 :], passed[: HEAD // 2]], axis=0)
+                turn_grad = passed * cos_turned - swapped * sin_turned
+                query = heads[rows, here].T.astype(F32)
+                scale = lax.rsqrt(jnp.mean(query * query, axis=0, keepdims=True) + EPSILON)
+                scaled = query * scale
+                s["q_gain_sum"][...] = s["q_gain_sum"][...] + turn_grad * scaled
+                inner = turn_grad * gain_turned
+                query_grad = scale * (inner - scaled * jnp.mean(inner * scaled, axis=0, keepdims=True))
+                heads[rows, here] = query_grad.astype(BF16).T
             turn_grad = unrotated(key_rot_grad * SCORE_SCALE, cos, sin)
             here = columns(8 + group, HEAD)
             key = heads[rows, here].astype(F32)
@@ -720,20 +744,18 @@
             add_gain(17, jnp.sum(turn_grad * key * scale, axis=0, keepdims=True))
             heads[rows, here] = norm_back(turn_grad, key, scale, k_gain[...]).astype(BF16)
             heads[rows, columns(12 + group, HEAD)] = value_grad.astype(BF16)
-            return carry
-
-        lax.fori_loop(0, 4, attend_back, 0)
-
-        def normed_back(part, carry):
-            value = dot(heads[rows, columns(0)], weight_part(QUERY, part), NT)
-            for k in (1, 2, 3):
-                value = value + dot(heads[rows, columns(k)], weight_part(QUERY + k, part), NT)
+
+        for index in range(4):
+            attend_back(index)
+
+        def normed_back(part):
+            value = times_back(heads[rows, :2048], range(QUERY, OUT), part)
             pair_start(1, part, value)
-            scaled = hidden[rows, columns(part, 256)].astype(F32) * scale_one[rows, :1]
+            scaled = hidden[rows, columns(part)].astype(F32) * scale_one[rows, :1]
             add_gains(0, part, jnp.sum(value * scaled, axis=0, keepdims=True))
-            return carry
-
-        lax.fori_loop(0, 4, normed_back, 0)
+
+        for index in range(2):
+            normed_back(index)
         pair_wait(1)
 
         def hidden_back_end(at, block):
@@ -754,11 +776,12 @@
 
     lax.fori_loop(0, 2, backward, 0)
 
-    turn(0, normed)
-    turn(1, attended_grad)
+    add_gain(16, jnp.sum(s["q_gain_sum"][...].T, axis=0, keepdims=True))
+    turn(2, normed)
+    turn(3, attended_grad)
 
     def attention_grad(chunk, carry):
-        weight_grad(MLP_CHUNKS + chunk, chunk // 4, heads[:, columns(chunk)])
+        weight_grad(MLP_CHUNKS + chunk, 2 + chunk // 4, heads[:, columns(chunk)])
         ring_start(MLP_CHUNKS + chunk)
         return carry
 

time: 233 us -> 208 us (0.89)
  Pallas kernels: 223 us -> 198 us
    pallas_call x1, Pallas kernels: 223 us -> 198 us  [shards(): pl.pallas_call(kernel, out_shape=(full, full, jax.ShapeDtypeStruct((CHUNK...]
where the time goes in v2:
time: 208 us
  Pallas kernels  198 us (95%)
  local copies, waits for them, and re-layouts  6.89 us (3%)
  other arithmetic  2.18 us (1%)
    pallas_call x1, Pallas kernels, shards(): pl.pallas_call(kernel, out_shape=(full, full, jax.ShapeDtypeStruct((CHUNK...  198 us

profile of v2, /device:TPU:0, one launch (start us, length us, event | category | flops | bytes accessed | tf_op | source)
XLA Modules:
  0.0 208.2 jit_solution(1439063415414277872)
XLA Ops:
  0.7 198.4 %shard_map.246 = (f32[512,1024]{1,0:T(8,128)}, f32[512,1024]{1,0:T(8,128)}, f32[15,32,512]{2,1,0:T(8,128)}, f32[24,128]{1,0:T(8,128)}) custom-call(s32[2,4]{1,0:T(2,128)} %lengths.1, bf16[512,1024]{1,0:T(8,128)(2,1)} %block_input.1, bf16[512,1024]{1,0:T(8,128)(2,1)} %cotangent.1, f32[1,1024]{1,0:T(1,128)} %attn_gain.1, f32[1,128]{1,0:T(1,128)} %q_gain.1, ...), custom_call_target="tpu_custom_call" | custom-call | tf_op jit(solution)/shard_map/pallas_call | solution.py:856
  199.1 0.0 copy-start.2
  199.1 0.0 copy-start.1
  199.1 2.1 %slice_bitcast_fusion.2 = (f32[32,512]{1,0:T(8,128)S(1)}, f32[32,512]{1,0:T(8,128)S(1)}, f32[32,512]{1,0:T(8,128)S(1)}, f32[32,512]{1,0:T(8,128)S(1)}, f32[32,51...) fusion(f32[15,32,512]{2,1,0:T(8,128)} %get-tuple-element.20), kind=kLoop, calls=%fused_computation.7 | loop fusion | bytes 1966080 | tf_op jit(solution)/shard_map/squeeze | solution.py:889
  201.2 0.8 maximum_bitcast_fusion
  202.0 0.7 maximum_bitcast_fusion.3
  202.7 0.7 maximum_bitcast_fusion.2
  203.4 0.0 copy-done.2
  203.4 0.6 fusion
  204.0 0.5 fusion.1
  204.5 0.0 copy-done.1
  204.5 0.0 copy-start
  204.5 1.3 copy.30
  205.8 1.0 copy-done
  206.8 1.3 copy.31
Async XLA Ops:
  199.1 4.3 %copy-start.2 = (f32[24,128]{1,0:T(8,128)S(1)}, f32[24,128]{1,0:T(8,128)}, u32[]{:S(2)}) copy-start(f32[24,128]{1,0:T(8,128)} %get-tuple-element.19) | copy-start | bytes 36868
  199.1 5.4 %copy-start.1 = (f32[512,1024]{1,0:T(8,128)S(1)}, f32[512,1024]{1,0:T(8,128)}, u32[]{:S(2)}) copy-start(f32[512,1024]{1,0:T(8,128)} %get-tuple-element.17) | copy-start | bytes 6291460
  204.5 2.3 %copy-start = (f32[512,1024]{1,0:T(8,128)S(1)}, f32[512,1024]{1,0:T(8,128)}, u32[]{:S(2)}) copy-start(f32[512,1024]{1,0:T(8,128)} %get-tuple-element.18) | copy-start | bytes 6291460

commit v3 on v2

--- a/solution.py
+++ b/solution.py
@@ -22,12 +22,16 @@
 TN = (((0,), (0,)), ((), ()))
 
 CHUNK = 512
-GATE, UP, DOWN, QUERY, KEY, VALUE, OUT = 0, 3, 6, 9, 11, 12, 13
+DOWN, GATE, UP, QUERY, KEY, VALUE, OUT = 0, 3, 6, 9, 11, 12, 13
 CHUNKS = 15
 MLP_CHUNKS = 9
 ORDERS = (("z", "y", "x"), ("y", "z", "x"))
 COUNTS = (8, 7)
 LAGS = (0, 0, 2, 2, 4, 6, 6, 8)
+LEFT = 3
+LEFT_ORDER = ("x", "y", "z")
+LEFT_LAGS = (0, 0, 1, 2, 2, 3, 4)
+LEFT_FROM = 6
 GAIN_ROWS = 24
 
 
@@ -62,19 +66,20 @@
     found, done = [], []
     for axis in order:
         left = [name for name in ("z", "x", "y") if name not in done and name != axis]
-        halved = None if axis == "x" else "x" if "x" in left else left[0]
+        halved = None if axis == "x" else "x" if "x" in left else left[0] if left else "row"
         shape = []
         for name in left:
             size = 2 if name == "x" else 4
             shape.append(size // 2 if name == halved else size)
-        found.append((axis, tuple(done), halved, (*shape, 32, CHUNK)))
+        rows = 16 if halved == "row" else 32
+        found.append((axis, tuple(done), halved, (*shape, rows, CHUNK)))
         done.append(axis)
     return found
 
 
-def ring_scratch(order, count):
+def ring_scratch(order, count, skipped=0):
     found = []
-    for _, _, halved, shape in ring_phases(order):
+    for _, _, halved, shape in ring_phases(order)[skipped:]:
         parts = 6 if halved else 1
         found.append(pltpu.VMEM((count, parts, *shape), BF16))
         found.append(pltpu.SemaphoreType.DMA((count, parts)))
@@ -82,15 +87,18 @@
     return found
 
 
-def ring_stages(order, grads, first, scratch, place, finish):
+def ring_stages(order, grads, at_first, scratch, place, finish, skipped=()):
     stages = []
-    for step, (axis, done, halved, _) in enumerate(ring_phases(order)):
+    phases = ring_phases(order)[len(skipped) :]
+    for step, (axis, done, halved, _) in enumerate(phases):
         arrived, send_sem, recv_sem = scratch[3 * step : 3 * step + 3]
         mine = place.at[axis]
 
         def where(i, index, half, axis=axis, done=done, halved=halved):
-            found = [2 * i + first]
+            found = list(at_first(i))
             for name in ("z", "x", "y"):
+                if name in skipped:
+                    continue
                 if name in done:
                     found.append(place.at[name])
                 elif name == axis:
@@ -100,11 +108,13 @@
                     found.append(pl.ds(half * size, size))
                 else:
                     found.append(slice(None))
+            if halved == "row":
+                found.append(pl.ds(half * 16, 16))
             return tuple(found)
 
         def put(i, half, total, step=step, mine=mine, where=where):
-            if step == 2:
-                finish(2 * i + first, total)
+            if step == len(phases) - 1:
+                finish(i, half, total)
             else:
                 grads[where(i, mine, half)] = total.astype(BF16)
 
@@ -227,7 +237,11 @@
             total = slots[0]
             for k in range(1, size):
                 total = total + slots[k]
-            dst[...] = total
+            if dst is total_ref:
+                for k in range(GAIN_ROWS):
+                    dst[:, k * 128 : (k + 1) * 128] = total[k : k + 1]
+            else:
+                dst[...] = total
 
         stages += [start, end]
     return stages
@@ -242,11 +256,11 @@
     key_rot=pltpu.VMEM((2 * ROW, 512), BF16),
     middle=pltpu.VMEM((2 * ROW, WIDTH), F32),
     normed_two=pltpu.VMEM((2 * ROW, WIDTH), BF16),
-    ff=pltpu.VMEM((3, 2 * ROW, 1536), BF16),
+    ff=pltpu.VMEM((3, 3, 4, 4, 32, CHUNK), BF16),
     grad=pltpu.VMEM((2 * ROW, WIDTH), BF16),
     attended_grad=pltpu.VMEM((2 * ROW, WIDTH), BF16),
     mixed_grad=pltpu.VMEM((ROW, 1024), BF16),
-    turned=pltpu.VMEM((4, 4, 2, 4, 32, CHUNK), BF16),
+    turned=pltpu.VMEM((2, 4, 2, 4, 32, CHUNK), BF16),
     mine=pltpu.VMEM((2, 2, ROW, CHUNK), BF16),
     theirs=pltpu.VMEM((2, 2, ROW, CHUNK), BF16),
     leaving=pltpu.VMEM((2 * ROW, WIDTH), BF16),
@@ -271,6 +285,13 @@
     cross_recv=pltpu.SemaphoreType.DMA((2, 2)),
     relay_send=pltpu.SemaphoreType.DMA((2, 2)),
     relay_recv=pltpu.SemaphoreType.DMA((2, 2)),
+    left_send=pltpu.SemaphoreType.DMA((LEFT, 2)),
+    left_recv=pltpu.SemaphoreType.DMA((LEFT, 2)),
+    left_sum=pltpu.VMEM((LEFT, 32, CHUNK), F32),
+    left_done=pltpu.VMEM((LEFT, 32, CHUNK), F32),
+    done_send=pltpu.SemaphoreType.DMA((LEFT,)),
+    done_recv=pltpu.SemaphoreType.DMA((LEFT,)),
+    left_free=pltpu.SemaphoreType.REGULAR,
 )
 
 
@@ -283,6 +304,7 @@
         body(
             pl.ds(pl.multiple_of(micro * ROW + block * BLOCK, BLOCK), BLOCK),
             pl.ds(block * BLOCK, BLOCK),
+            (2 * micro + block // 4, block % 4),
         )
 
 
@@ -330,6 +352,7 @@
     place = Place()
     section, tensor = lax.axis_index("section"), lax.axis_index("tensor")
     over_tensor, over_section = {"tensor": 1 - tensor}, {"section": 1 - section}
+    aslant = {"section": 1 - section, **place.device("x", 1 - place.at["x"])}
 
     barrier = pltpu.get_barrier_semaphore()
     for size, own, device in gain_axes(place):
@@ -337,11 +360,12 @@
             pl.semaphore_signal(
                 barrier, inc=1, device_id=device(lax.rem(own + k, size)), device_id_type=MESH
             )
-    pl.semaphore_signal(barrier, inc=1, device_id=over_section, device_id_type=MESH)
+    for device in (over_section, aslant):
+        pl.semaphore_signal(barrier, inc=1, device_id=device, device_id_type=MESH)
 
     sources = (
         [(q_weight, 0), (q_weight, 1), (key_matrix, 0), (value_matrix, 0), (o_weight, 0), (o_weight, 1)],
-        [(ref, k) for ref in (gate_weight, up_weight, down_weight) for k in range(3)],
+        [(ref, k) for ref in (down_weight, gate_weight, up_weight) for k in range(3)],
     )
 
     def load(chunk):
@@ -363,7 +387,7 @@
         load_input(0).start()
         load_input(1).start()
 
-    for chunk in (9, 10, 11, 12, 13, 14, 0, 3, 1, 4, 2, 5, 6, 7, 8):
+    for chunk in (9, 10, 11, 12, 13, 14, 3, 6, 4, 7, 5, 8, 0, 1, 2):
         load(chunk).start()
 
     @pl.when(section == 1)
@@ -404,7 +428,7 @@
     s["q_gain_turned"][...] = jnp.broadcast_to(q_gain[...], (HEAD, HEAD)).T
     s["q_gain_sum"][...] = jnp.zeros((HEAD, ROW), F32)
 
-    pl.semaphore_wait(barrier, 9)
+    pl.semaphore_wait(barrier, 10)
 
     def pair(slot, part):
         return remote(
@@ -472,6 +496,10 @@
         right = [weights[chunk, 2 * part : 2 * part + 2].reshape(CHUNK, CHUNK) for chunk in chunks]
         return dot(left, jnp.concatenate(right, axis=1), NT)
 
+    def units(micro, *slots):
+        found = [ff[slot, k, pl.ds(2 * micro, 2)].reshape(ROW, CHUNK) for slot in slots for k in range(3)]
+        return jnp.concatenate(found, axis=1)
+
     def once(micro, chunks):
         @pl.when(micro == 0)
         def _():
@@ -495,7 +523,7 @@
         def _():
             arrive(0, micro)
 
-        def norm_one(at, block):
+        def norm_one(at, block, _):
             value = hidden[at].astype(F32)
             scale = inverse_rms(value)
             normed[at] = (value * scale * attn_gain[...]).astype(BF16)
@@ -544,7 +572,7 @@
 
         pair_wait(0)
 
-        def norm_two(at, block):
+        def norm_two(at, block, _):
             value = hidden[at].astype(F32) + pair_sum(0, block)
             middle[at] = value
             scale = inverse_rms(value)
@@ -558,11 +586,11 @@
             wide[0] = dot(normed_two[rows], weight(GATE + chunk))
             wide[1] = dot(normed_two[rows], weight(UP + chunk))
 
-            def silu(at, block):
+            def silu(at, block, place_in):
                 gate, up = wide[0, block], wide[1, block]
-                ff[0, at, columns(chunk)] = gate.astype(BF16)
-                ff[1, at, columns(chunk)] = up.astype(BF16)
-                ff[2, at, columns(chunk)] = (gate * jax.nn.sigmoid(gate) * up).astype(BF16)
+                ff[1, chunk, *place_in] = gate.astype(BF16)
+                ff[2, chunk, *place_in] = up.astype(BF16)
+                ff[0, chunk, *place_in] = (gate * jax.nn.sigmoid(gate) * up).astype(BF16)
 
             over_rows(micro, silu)
 
@@ -570,7 +598,7 @@
             hidden_units(index)
 
         def moved(part):
-            value = times_back(ff[2, rows], range(DOWN, QUERY), part)
+            value = times_back(units(micro, 0), range(DOWN, GATE), part)
             pair_start(1, part, value)
 
         for index in range(2):
@@ -578,7 +606,7 @@
 
         pair_wait(1)
 
-        def result(at, block):
+        def result(at, block, _):
             value = middle[at] + pair_sum(1, block)
             stage[at] = value
             leaving[at] = value.astype(BF16)
@@ -614,29 +642,82 @@
 
     @pl.when(section == 0)
     def _():
-        turn(0, normed_two)
+        turn(1, normed_two)
 
     def weight_grad(chunk, slot, right):
         for part in range(4):
             value = dot(turned[slot, part].reshape(256, CHUNK), right)
             weights[chunk, part] = value.astype(BF16).reshape(2, 4, 32, CHUNK)
 
-    def finish(chunk, total):
-        if total.shape[0] == 1:
-            total = total[0]
-        grads_out[chunk] = total
-
     rings = []
     for first, (order, count) in enumerate(zip(ORDERS, COUNTS)):
         own, scratch = scratch[:9], scratch[9:]
-        rings.append((count, LAGS, ring_stages(order, weights, first, own, place, finish)))
+
+        def finish(i, half, total, first=first):
+            grads_out[2 * i + first] = total
+
+        def chunk_at(i, first=first):
+            return (2 * i + first,)
+
+        rings.append((count, LAGS, ring_stages(order, weights, chunk_at, own, place, finish)))
+
+    def kept(chunk):
+        return (section == 1) | (lax.rem(chunk, 3) > 0) | (chunk >= MLP_CHUNKS)
 
     def ring_start(chunk):
         for first in (0, 1):
 
-            @pl.when(lax.rem(chunk, 2) == first)
+            @pl.when((lax.rem(chunk, 2) == first) & kept(chunk))
             def _(first=first):
                 rings[first][2][0]((chunk - first) // 2)
+
+        @pl.when(jnp.logical_not(kept(chunk)))
+        def _():
+            leave(chunk // 3, 0).start()
+            leave(chunk // 3, 1).start()
+
+    def leave(i, slant):
+        side = place.at["x"]
+        return remote(
+            weights.at[3 * i, :, 1 - side if slant else side],
+            ff.at[i, side],
+            s["left_send"].at[i, slant],
+            s["left_recv"].at[i, side],
+            aslant if slant else over_section,
+        )
+
+    def left_arrival(i, side):
+        return remote(
+            weights.at[3 * i, :, side],
+            ff.at[i, side],
+            s["left_send"].at[i, side],
+            s["left_recv"].at[i, side],
+            over_section,
+        )
+
+    def give_back(i):
+        return remote(
+            s["left_sum"].at[i],
+            s["left_done"].at[i],
+            s["done_send"].at[i],
+            s["done_recv"].at[i],
+            over_section,
+        )
+
+    def left_start(i):
+        for side in (0, 1):
+            left_arrival(i, side).wait_recv()
+        ff[i, 2] = (ff[i, 0].astype(F32) + ff[i, 1].astype(F32)).astype(BF16)
+
+    def left_finish(i, half, total):
+        s["left_sum"][i, half * 16 : half * 16 + 16] = total
+        if half:
+            give_back(i).start()
+
+    own, scratch = scratch[:6], scratch[6:]
+    left_stages = [left_start] + ring_stages(
+        LEFT_ORDER, ff, lambda i: (i, 2), own, place, left_finish, skipped=("x",)
+    )
 
     def backward(micro, carry):
         rows = rows_of(micro)
@@ -653,13 +734,13 @@
         def hidden_back(chunk):
             wide[0] = dot(grad[rows], weight(DOWN + chunk))
 
-            def silu_back(at, block):
+            def silu_back(at, block, place_in):
                 act_grad = wide[0, block]
-                gate, up = ff[0, at, columns(chunk)].astype(F32), ff[1, at, columns(chunk)].astype(F32)
+                gate, up = ff[1, chunk, *place_in].astype(F32), ff[2, chunk, *place_in].astype(F32)
                 sigma = jax.nn.sigmoid(gate)
                 passed = act_grad * sigma
-                ff[0, at, columns(chunk)] = (passed * up * (1.0 + gate * (1.0 - sigma))).astype(BF16)
-                ff[1, at, columns(chunk)] = (passed * gate).astype(BF16)
+                ff[1, chunk, *place_in] = (passed * up * (1.0 + gate * (1.0 - sigma))).astype(BF16)
+                ff[2, chunk, *place_in] = (passed * gate).astype(BF16)
 
             over_rows(micro, silu_back)
 
@@ -667,18 +748,48 @@
             hidden_back(index)
 
         def normed_two_back(part):
-            left = jnp.concatenate([ff[0, rows], ff[1, rows]], axis=1)
-            value = times_back(left, range(GATE, DOWN), part)
+            value = times_back(units(micro, 1, 2), range(GATE, QUERY), part)
             pair_start(0, part, value)
             scaled = middle[rows, columns(part)] * scale_two[rows, :1]
             add_gains(8, part, jnp.sum(value * scaled, axis=0, keepdims=True))
 
+        def mlp_grad(chunk, carry):
+            weight_grad(chunk, jnp.minimum(chunk // 3, 1), ff[chunk // 3, lax.rem(chunk, 3)].reshape(2 * ROW, CHUNK))
+            ring_start(chunk)
+            return carry
+
+        @pl.when(micro == 1)
+        def _():
+            turn(0, grad)
+
+            @pl.when(section == 0)
+            def _():
+                pl.semaphore_wait(s["left_free"], 2)
+
+            lax.fori_loop(DOWN, GATE, mlp_grad, 0)
+
         for index in range(2):
             normed_two_back(index)
+
+        @pl.when(micro == 1)
+        def _():
+            @pl.when(section == 1)
+            def _():
+                turn(1, normed_two)
+
+            lax.fori_loop(GATE, QUERY, mlp_grad, 0)
+
+            @pl.when(section == 1)
+            def _():
+                for device in (over_section, aslant):
+                    pl.semaphore_signal(
+                        s["left_free"], inc=1, device_id=device, device_id_type=MESH
+                    )
+
         pair_wait(0)
         output(0, micro).wait()
 
-        def middle_back(at, block):
+        def middle_back(at, block, _):
             value = grad[at].astype(F32) + norm_back(
                 pair_sum(0, block), middle[at], scale_two[at, :1], mlp_gain[...]
             )
@@ -686,21 +797,6 @@
             attended_grad[at] = value.astype(BF16)
 
         over_rows(micro, middle_back)
-
-        @pl.when(micro == 1)
-        def _():
-            @pl.when(section == 1)
-            def _():
-                turn(0, normed_two)
-
-            def one(chunk, carry):
-                weight_grad(chunk, chunk // 6, ff[chunk // 3, :, columns(lax.rem(chunk, 3))])
-                ring_start(chunk)
-                return carry
-
-            lax.fori_loop(0, DOWN, one, 0)
-            turn(1, grad)
-            lax.fori_loop(DOWN, MLP_CHUNKS, one, 0)
 
         for k in range(2):
             mixed_grad[:, columns(k)] = dot(attended_grad[rows], weight(OUT + k)).astype(BF16)
@@ -758,7 +854,7 @@
             normed_back(index)
         pair_wait(1)
 
-        def hidden_back_end(at, block):
+        def hidden_back_end(at, block, _):
             value = stage[at] + norm_back(
                 pair_sum(1, block), hidden[at].astype(F32), scale_one[at, :1], attn_gain[...]
             )
@@ -777,33 +873,55 @@
     lax.fori_loop(0, 2, backward, 0)
 
     add_gain(16, jnp.sum(s["q_gain_sum"][...].T, axis=0, keepdims=True))
-    turn(2, normed)
-    turn(3, attended_grad)
+    turn(0, normed)
+    turn(1, attended_grad)
 
     def attention_grad(chunk, carry):
-        weight_grad(MLP_CHUNKS + chunk, 2 + chunk // 4, heads[:, columns(chunk)])
+        weight_grad(MLP_CHUNKS + chunk, chunk // 4, heads[:, columns(chunk)])
         ring_start(MLP_CHUNKS + chunk)
         return carry
 
     lax.fori_loop(0, CHUNKS - MLP_CHUNKS, attention_grad, 0)
 
-    groups = [(count, (None, *lags[1:]), stages) for count, lags, stages in rings]
-    groups.append((1, (0, 2, 2, 4, 4, 6, 6, 8), gain_stages(gains_out, scratch, place)))
+    def always(i):
+        return True
+
+    groups = [
+        (count, (None, *lags[1:]), stages, lambda i, first=first: kept(2 * i + first))
+        for first, (count, lags, stages) in enumerate(rings)
+    ]
+    groups.append(
+        (LEFT, [LEFT_FROM + lag for lag in LEFT_LAGS], left_stages, lambda i: section == 1)
+    )
+    groups.append((1, (0, 2, 2, 4, 4, 6, 6, 8), gain_stages(gains_out, scratch, place), always))
 
     def advance(now, carry):
         for step in range(8):
-            for count, lags, stages in groups:
-                if lags[step] is None:
+            for count, lags, stages, runs in groups:
+                if step >= len(stages) or lags[step] is None:
                     continue
                 i = now - lags[step]
 
-                @pl.when((i >= 0) & (i < count))
+                @pl.when((i >= 0) & (i < count) & runs(i))
                 def _(i=i, run=stages[step]):
                     run(i)
 
         return carry
 
-    lax.fori_loop(0, max(count + lags[-1] for count, lags, _ in groups), advance, 0)
+    lax.fori_loop(0, max(count + lags[-1] for count, lags, _, _ in groups), advance, 0)
+
+    @pl.when(section == 0)
+    def _():
+        for i in range(LEFT):
+            leave(i, 0).wait_send()
+            leave(i, 1).wait_send()
+            give_back(i).wait_recv()
+            grads_out[3 * i] = s["left_done"][i]
+
+    @pl.when(section == 1)
+    def _():
+        for i in range(LEFT):
+            give_back(i).wait_send()
 
     for micro in range(2):
         output(1, micro).wait()
@@ -851,6 +969,7 @@
     scratch = list(SCRATCH.values())
     for order, count in zip(ORDERS, COUNTS):
         scratch += ring_scratch(order, count)
+    scratch += ring_scratch(LEFT_ORDER, LEFT, 1)
     scratch += gain_scratch()
     full = jax.ShapeDtypeStruct(block_input.shape, F32)
     outputs, grads_in, grads, gains = pl.pallas_call(
@@ -859,7 +978,7 @@
             full,
             full,
             jax.ShapeDtypeStruct((CHUNKS, 32, CHUNK), F32),
-            jax.ShapeDtypeStruct((GAIN_ROWS, 128), F32),
+            jax.ShapeDtypeStruct((1, GAIN_ROWS * 128), F32),
         ),
         in_specs=[smem, anywhere, anywhere] + [vmem] * 4 + [anywhere] * 7 + [vmem],
         out_specs=[anywhere, anywhere, vmem, vmem],
@@ -885,25 +1004,62 @@
         rope_table(),
     )
 
-    def matrix(first, count):
-        return jnp.concatenate([grads[first + k] for k in range(count)], axis=1)[None]
-
-    flat = gains.reshape(1, -1)
-    return (
-        outputs[None],
-        grads_in[None],
-        flat[:, :1024],
-        flat[:, 2048:2176],
-        flat[:, 2176:2304],
-        flat[:, 1024:2048],
-        matrix(QUERY, 2),
-        matrix(KEY, 1),
-        matrix(VALUE, 1),
-        matrix(OUT, 2),
-        matrix(GATE, 3),
-        matrix(UP, 3),
-        matrix(DOWN, 3),
-    )
+    return spread(outputs, grads_in, grads, gains)
+
+
+MATRICES = ((QUERY, 2), (KEY, 1), (VALUE, 1), (OUT, 2), (GATE, 3), (UP, 3), (DOWN, 3))
+GAIN_PARTS = ((0, 1024), (2048, 128), (2176, 128), (1024, 1024))
+
+
+def spread_kernel(outputs, grads_in, grads, gains, *refs):
+    results, (tokens, matrices, row, in_sem, out_sem) = refs[:-5], refs[-5:]
+    loads, stores = [], []
+
+    def through(src, held, pairs):
+        load = pltpu.make_async_copy(src, held, in_sem.at[len(loads)])
+        load.start()
+        loads.append((load, pairs))
+
+    through(grads, matrices, [])
+    for k in range(8):
+        rows = pl.ds(k % 4 * 128, 128)
+        src, into = ((outputs, results[0]), (grads_in, results[1]))[k // 4]
+        through(src.at[rows], tokens.at[k], [(tokens.at[k], into.at[0, rows])])
+    through(gains, row, [])
+    for (first, count), into in zip(MATRICES, results[6:]):
+        for k in range(count):
+            pair = (matrices.at[first + k], into.at[0, :, k * CHUNK : (k + 1) * CHUNK])
+            loads[0][1].append(pair)
+    for (first, size), into in zip(GAIN_PARTS, results[2:6]):
+        loads[-1][1].append((row.at[:, first : first + size], into))
+    for load, pairs in loads:
+        load.wait()
+        for src, dst in pairs:
+            store = pltpu.make_async_copy(src, dst, out_sem.at[len(stores)])
+            store.start()
+            stores.append(store)
+    for store in stores:
+        store.wait()
+
+
+def spread(outputs, grads_in, grads, gains):
+    shapes = [(1, *outputs.shape)] * 2 + [(1, size) for _, size in GAIN_PARTS]
+    shapes += [(1, 32, count * CHUNK) for _, count in MATRICES]
+    anywhere = pl.BlockSpec(memory_space=pl.ANY)
+    return pl.pallas_call(
+        spread_kernel,
+        out_shape=[jax.ShapeDtypeStruct(shape, F32) for shape in shapes],
+        in_specs=[anywhere] * 4,
+        out_specs=[anywhere] * len(shapes),
+        scratch_shapes=[
+            pltpu.VMEM((8, 128, outputs.shape[1]), F32),
+            pltpu.VMEM(grads.shape, F32),
+            pltpu.VMEM(gains.shape, F32),
+            pltpu.SemaphoreType.DMA((10,)),
+            pltpu.SemaphoreType.DMA((27,)),
+        ],
+        compiler_params=pltpu.CompilerParams(vmem_limit_bytes=16 * 2**20),
+    )(outputs, grads_in, grads, gains)
 
 
 def solution(mesh):

time: 208 us -> 187 us (0.90)
  Pallas kernels: 198 us -> 180 us
  other arithmetic: 2.18 us -> 0 us
    pallas_call x1, Pallas kernels: 198 us -> 177 us  [shards(): pl.pallas_call(kernel, out_shape=(full, full, jax.ShapeDtypeStruct((CHUNK...]
    pallas_call x0 -> x1, Pallas kernels: none -> 3.26 us  [spread(): pl.pallas_call(spread_kernel, out_shape=[jax.ShapeDtypeStruct(shape, F32)...]
    broadcast_in_dim x3 -> x0, other arithmetic: 2.18 us -> none  [matrix(): jnp.concatenate([grads[first + k] for k in range(count)], axis=1)[None]]
    squeeze x1 -> x0, local copies, waits for them, and re-layouts: 2.1 us -> none  [matrix(): grads[first + k]]
where the time goes in v3:
time: 187 us; the launch traced here: 186 us
  Pallas kernels  180 us (96%)
  local copies, waits for them, and re-layouts  5.08 us (3%)
    pallas_call x1, Pallas kernels, shards(): pl.pallas_call(kernel, out_shape=(full, full, jax.ShapeDtypeStruct((CHUNK...  177 us
    unnamed x8, local copies, waits for them, and re-layouts  5.08 us

profile of v3, /device:TPU:0, one launch (start us, length us, event | category | flops | bytes accessed | tf_op | source)
XLA Modules:
  0.0 186.3 jit_solution(6142874642144787127)
XLA Ops:
  0.7 177.1 %shard_map.246 = (f32[512,1024]{1,0:T(8,128)}, f32[512,1024]{1,0:T(8,128)}, f32[15,32,512]{2,1,0:T(8,128)}, f32[1,3072]{1,0:T(1,128)}) custom-call(s32[2,4]{1,0:T(2,128)} %lengths.1, bf16[512,1024]{1,0:T(8,128)(2,1)} %block_input.1, bf16[512,1024]{1,0:T(8,128)(2,1)} %cotangent.1, f32[1,1024]{1,0:T(1,128)} %attn_gain.1, f32[1,128]{1,0:T(1,128)} %q_gain.1, ...), custom_call_target="tpu_custom_call" | custom-call | tf_op jit(solution)/shard_map/pallas_call | solution.py:975
  177.8 0.0 copy-start
  177.8 1.6 copy-done
  179.4 0.0 copy-start.1
  179.4 1.6 copy-done.1
  181.0 0.0 copy-start.2
  181.0 1.2 copy-done.2
  182.2 0.0 copy-start.3
  182.2 0.7 copy-done.3
  182.9 3.3 %shard_map.247 = (f32[1,512,1024]{2,1,0:T(8,128)}, f32[1,512,1024]{2,1,0:T(8,128)}, f32[1,1024]{1,0:T(1,128)}, f32[1,128]{1,0:T(1,128)}, f32[1,128]{1,0:T(1,128)...) custom-call(f32[512,1024]{1,0:T(8,128)S(1)} %copy-done, ...), custom_call_target="tpu_custom_call" | custom-call | tf_op jit(solution)/shard_map/pallas_call | solution.py:1049
Async XLA Ops:
  177.8 1.6 copy-start
  179.4 1.6 copy-start.1
  181.0 1.2 copy-start.2
  182.2 0.7 copy-start.3

commit v4 on v3

--- a/solution.py
+++ b/solution.py
@@ -261,9 +261,9 @@
     attended_grad=pltpu.VMEM((2 * ROW, WIDTH), BF16),
     mixed_grad=pltpu.VMEM((ROW, 1024), BF16),
     turned=pltpu.VMEM((2, 4, 2, 4, 32, CHUNK), BF16),
-    mine=pltpu.VMEM((2, 2, ROW, CHUNK), BF16),
-    theirs=pltpu.VMEM((2, 2, ROW, CHUNK), BF16),
-    leaving=pltpu.VMEM((2 * ROW, WIDTH), BF16),
+    mine=pltpu.VMEM((4, 2, ROW, CHUNK), BF16),
+    theirs=pltpu.VMEM((4, 2, ROW, CHUNK), BF16),
+    leaving=pltpu.VMEM((2, ROW // 2, WIDTH), BF16),
     stage=pltpu.VMEM((2 * ROW, WIDTH), F32),
     cosine=pltpu.VMEM((2 * ROW, HEAD), F32),
     sine=pltpu.VMEM((2 * ROW, HEAD), F32),
@@ -279,8 +279,8 @@
     weight_sem=pltpu.SemaphoreType.DMA((CHUNKS,)),
     input_sem=pltpu.SemaphoreType.DMA((2,)),
     output_sem=pltpu.SemaphoreType.DMA((2, 2)),
-    mine_sem=pltpu.SemaphoreType.DMA((2, 2)),
-    theirs_sem=pltpu.SemaphoreType.DMA((2, 2)),
+    mine_sem=pltpu.SemaphoreType.DMA((4, 2)),
+    theirs_sem=pltpu.SemaphoreType.DMA((4, 2)),
     cross_send=pltpu.SemaphoreType.DMA((2, 2)),
     cross_recv=pltpu.SemaphoreType.DMA((2, 2)),
     relay_send=pltpu.SemaphoreType.DMA((2, 2)),
@@ -463,7 +463,7 @@
         rows = half_rows(micro)
         into = hidden if way == 0 else grad
         return remote(
-            leaving.at[rows],
+            leaving.at[micro],
             into.at[rows],
             s["cross_send"].at[way, micro],
             s["cross_recv"].at[way, micro],
@@ -484,6 +484,11 @@
         relay.start()
         relay.wait()
 
+    def pack(micro):
+        for block in range(ROW // 2 // BLOCK):
+            at = pl.multiple_of(micro * ROW + tensor * (ROW // 2) + block * BLOCK, BLOCK)
+            leaving[micro, block * BLOCK : (block + 1) * BLOCK] = stage[pl.ds(at, BLOCK)].astype(BF16)
+
     def output(way, micro):
         rows = rows_of(micro)
         into = hidden_out if way == 0 else hidden_grad
@@ -512,7 +517,7 @@
     def unrotated(value, cos, sin):
         return value * cos - pltpu.roll(value, HEAD // 2, 1) * sin
 
-    def forward(micro, carry):
+    def forward_one(micro):
         rows = rows_of(micro)
 
         @pl.when(section == 0)
@@ -570,6 +575,8 @@
         for index in range(2):
             attended(index)
 
+    def forward_two(micro):
+        rows = rows_of(micro)
         pair_wait(0)
 
         def norm_two(at, block, _):
@@ -604,23 +611,19 @@
         for index in range(2):
             moved(index)
 
+    def forward_three(micro):
         pair_wait(1)
 
         def result(at, block, _):
-            value = middle[at] + pair_sum(1, block)
-            stage[at] = value
-            leaving[at] = value.astype(BF16)
+            stage[at] = middle[at] + pair_sum(1, block)
 
         over_rows(micro, result)
         output(0, micro).start()
 
         @pl.when(section == 0)
         def _():
+            pack(micro)
             cross(0, micro).start()
-
-        return carry
-
-    lax.fori_loop(0, 2, forward, 0)
 
     def norm_back(total, value, scale, gain):
         inner = total * gain
@@ -639,10 +642,6 @@
     def turn(slot, value):
         for k in range(4):
             turned[slot, k] = value[:, columns(k, 256)].T.reshape(2, 4, 32, CHUNK)
-
-    @pl.when(section == 0)
-    def _():
-        turn(1, normed_two)
 
     def weight_grad(chunk, slot, right):
         for part in range(4):
@@ -719,7 +718,7 @@
         LEFT_ORDER, ff, lambda i: (i, 2), own, place, left_finish, skipped=("x",)
     )
 
-    def backward(micro, carry):
+    def backward_one(micro):
         rows = rows_of(micro)
 
         @pl.when(section == 0)
@@ -749,7 +748,7 @@
 
         def normed_two_back(part):
             value = times_back(units(micro, 1, 2), range(GATE, QUERY), part)
-            pair_start(0, part, value)
+            pair_start(2, part, value)
             scaled = middle[rows, columns(part)] * scale_two[rows, :1]
             add_gains(8, part, jnp.sum(value * scaled, axis=0, keepdims=True))
 
@@ -786,12 +785,14 @@
                         s["left_free"], inc=1, device_id=device, device_id_type=MESH
                     )
 
-        pair_wait(0)
+    def backward_two(micro):
+        rows = rows_of(micro)
+        pair_wait(2)
         output(0, micro).wait()
 
         def middle_back(at, block, _):
             value = grad[at].astype(F32) + norm_back(
-                pair_sum(0, block), middle[at], scale_two[at, :1], mlp_gain[...]
+                pair_sum(2, block), middle[at], scale_two[at, :1], mlp_gain[...]
             )
             stage[at] = value
             attended_grad[at] = value.astype(BF16)
@@ -846,31 +847,52 @@
 
         def normed_back(part):
             value = times_back(heads[rows, :2048], range(QUERY, OUT), part)
-            pair_start(1, part, value)
+            pair_start(3, part, value)
             scaled = hidden[rows, columns(part)].astype(F32) * scale_one[rows, :1]
             add_gains(0, part, jnp.sum(value * scaled, axis=0, keepdims=True))
 
         for index in range(2):
             normed_back(index)
-        pair_wait(1)
+    def backward_three(micro):
+        pair_wait(3)
 
         def hidden_back_end(at, block, _):
-            value = stage[at] + norm_back(
-                pair_sum(1, block), hidden[at].astype(F32), scale_one[at, :1], attn_gain[...]
+            stage[at] = stage[at] + norm_back(
+                pair_sum(3, block), hidden[at].astype(F32), scale_one[at, :1], attn_gain[...]
             )
-            stage[at] = value
-            leaving[at] = value.astype(BF16)
 
         over_rows(micro, hidden_back_end)
         output(1, micro).start()
 
         @pl.when(section == 1)
         def _():
+            pack(micro)
             cross(1, micro).start()
 
+    def step(turn_of, carry):
+        back = turn_of - 2 + section
+
+        @pl.when((turn_of == 2) & (section == 0))
+        def _():
+            turn(1, normed_two)
+
+        for ahead, behind in (
+            (forward_one, backward_one),
+            (forward_two, backward_two),
+            (forward_three, backward_three),
+        ):
+
+            @pl.when((back >= 0) & (back < 2))
+            def _(behind=behind):
+                behind(back)
+
+            @pl.when(turn_of < 2)
+            def _(ahead=ahead):
+                ahead(turn_of)
+
         return carry
 
-    lax.fori_loop(0, 2, backward, 0)
+    lax.fori_loop(0, 4, step, 0)
 
     add_gain(16, jnp.sum(s["q_gain_sum"][...].T, axis=0, keepdims=True))
     turn(0, normed)

time: 187 us -> 183 us (0.979)
  Pallas kernels: 180 us -> 176 us
    pallas_call x1, Pallas kernels: 177 us -> 173 us  [shards(): pl.pallas_call(kernel, out_shape=(full, full, jax.ShapeDtypeStruct((CHUNK...]
where the time goes in v4:
time: 183 us; the launch traced here: 182 us
  Pallas kernels  176 us (96%)
  local copies, waits for them, and re-layouts  5.08 us (3%)
    pallas_call x1, Pallas kernels, shards(): pl.pallas_call(kernel, out_shape=(full, full, jax.ShapeDtypeStruct((CHUNK...  173 us
    unnamed x8, local copies, waits for them, and re-layouts  5.08 us

profile of v4, /device:TPU:0, one launch (start us, length us, event | category | flops | bytes accessed | tf_op | source)
XLA Modules:
  0.0 182.2 jit_solution(5909256167768253872)
XLA Ops:
  0.7 173.1 %shard_map.246 = (f32[512,1024]{1,0:T(8,128)}, f32[512,1024]{1,0:T(8,128)}, f32[15,32,512]{2,1,0:T(8,128)}, f32[1,3072]{1,0:T(1,128)}) custom-call(s32[2,4]{1,0:T(2,128)} %lengths.1, bf16[512,1024]{1,0:T(8,128)(2,1)} %block_input.1, bf16[512,1024]{1,0:T(8,128)(2,1)} %cotangent.1, f32[1,1024]{1,0:T(1,128)} %attn_gain.1, f32[1,128]{1,0:T(1,128)} %q_gain.1, ...), custom_call_target="tpu_custom_call" | custom-call | tf_op jit(solution)/shard_map/pallas_call | solution.py:997
  173.7 0.0 copy-start
  173.7 1.6 copy-done
  175.3 0.0 copy-start.1
  175.3 1.6 copy-done.1
  176.9 0.0 copy-start.2
  176.9 1.2 copy-done.2
  178.1 0.0 copy-start.3
  178.1 0.7 copy-done.3
  178.8 3.3 %shard_map.247 = (f32[1,512,1024]{2,1,0:T(8,128)}, f32[1,512,1024]{2,1,0:T(8,128)}, f32[1,1024]{1,0:T(1,128)}, f32[1,128]{1,0:T(1,128)}, f32[1,128]{1,0:T(1,128)...) custom-call(f32[512,1024]{1,0:T(8,128)S(1)} %copy-done, ...), custom_call_target="tpu_custom_call" | custom-call | tf_op jit(solution)/shard_map/pallas_call | solution.py:1071
Async XLA Ops:
  173.7 1.6 copy-start
  175.3 1.6 copy-start.1
  176.9 1.2 copy-start.2
  178.1 0.7 copy-start.3

commit v5 on v4

--- a/solution.py
+++ b/solution.py
@@ -25,6 +25,7 @@
 DOWN, GATE, UP, QUERY, KEY, VALUE, OUT = 0, 3, 6, 9, 11, 12, 13
 CHUNKS = 15
 MLP_CHUNKS = 9
+SOON = 7
 ORDERS = (("z", "y", "x"), ("y", "z", "x"))
 COUNTS = (8, 7)
 LAGS = (0, 0, 2, 2, 4, 6, 6, 8)
@@ -263,7 +264,7 @@
     turned=pltpu.VMEM((2, 4, 2, 4, 32, CHUNK), BF16),
     mine=pltpu.VMEM((4, 2, ROW, CHUNK), BF16),
     theirs=pltpu.VMEM((4, 2, ROW, CHUNK), BF16),
-    leaving=pltpu.VMEM((2, ROW // 2, WIDTH), BF16),
+    leaving=pltpu.VMEM((2, 2, ROW // 2, CHUNK), BF16),
     stage=pltpu.VMEM((2 * ROW, WIDTH), F32),
     cosine=pltpu.VMEM((2 * ROW, HEAD), F32),
     sine=pltpu.VMEM((2 * ROW, HEAD), F32),
@@ -281,10 +282,10 @@
     output_sem=pltpu.SemaphoreType.DMA((2, 2)),
     mine_sem=pltpu.SemaphoreType.DMA((4, 2)),
     theirs_sem=pltpu.SemaphoreType.DMA((4, 2)),
-    cross_send=pltpu.SemaphoreType.DMA((2, 2)),
-    cross_recv=pltpu.SemaphoreType.DMA((2, 2)),
-    relay_send=pltpu.SemaphoreType.DMA((2, 2)),
-    relay_recv=pltpu.SemaphoreType.DMA((2, 2)),
+    cross_send=pltpu.SemaphoreType.DMA((2, 2, 2)),
+    cross_recv=pltpu.SemaphoreType.DMA((2, 2, 2)),
+    relay_send=pltpu.SemaphoreType.DMA((2, 2, 2)),
+    relay_recv=pltpu.SemaphoreType.DMA((2, 2, 2)),
     left_send=pltpu.SemaphoreType.DMA((LEFT, 2)),
     left_recv=pltpu.SemaphoreType.DMA((LEFT, 2)),
     left_sum=pltpu.VMEM((LEFT, 32, CHUNK), F32),
@@ -447,6 +448,9 @@
         for part in range(2):
             pair(slot, part).wait()
 
+    def pair_part(slot, part, block):
+        return mine[slot, part, block].astype(F32) + theirs[slot, part, block].astype(F32)
+
     def pair_sum(slot, block):
         return jnp.concatenate(
             [
@@ -459,35 +463,45 @@
     def half_rows(micro):
         return pl.ds(pl.multiple_of(micro * ROW + tensor * (ROW // 2), ROW // 2), ROW // 2)
 
-    def cross(way, micro):
-        rows = half_rows(micro)
+    def cross(way, micro, part):
         into = hidden if way == 0 else grad
         return remote(
-            leaving.at[micro],
-            into.at[rows],
-            s["cross_send"].at[way, micro],
-            s["cross_recv"].at[way, micro],
+            leaving.at[micro, part],
+            into.at[half_rows(micro), columns(part)],
+            s["cross_send"].at[way, micro, part],
+            s["cross_recv"].at[way, micro, part],
             over_section,
         )
 
+    def cross_sent(way, micro):
+        for part in range(2):
+            cross(way, micro, part).wait_send()
+
     def arrive(way, micro):
-        rows = half_rows(micro)
         into = hidden if way == 0 else grad
-        cross(way, micro).wait_recv()
-        relay = remote(
-            into.at[rows],
-            into.at[rows],
-            s["relay_send"].at[way, micro],
-            s["relay_recv"].at[way, micro],
-            over_tensor,
-        )
-        relay.start()
-        relay.wait()
-
-    def pack(micro):
+
+        def relay(part):
+            here = into.at[half_rows(micro), columns(part)]
+            return remote(
+                here,
+                here,
+                s["relay_send"].at[way, micro, part],
+                s["relay_recv"].at[way, micro, part],
+                over_tensor,
+            )
+
+        for part in range(2):
+            cross(way, micro, part).wait_recv()
+            relay(part).start()
+        for part in range(2):
+            relay(part).wait()
+
+    def leave_for(way, micro, part):
         for block in range(ROW // 2 // BLOCK):
             at = pl.multiple_of(micro * ROW + tensor * (ROW // 2) + block * BLOCK, BLOCK)
-            leaving[micro, block * BLOCK : (block + 1) * BLOCK] = stage[pl.ds(at, BLOCK)].astype(BF16)
+            value = stage[pl.ds(at, BLOCK), columns(part)]
+            leaving[micro, part, block * BLOCK : (block + 1) * BLOCK] = value.astype(BF16)
+        cross(way, micro, part).start()
 
     def output(way, micro):
         rows = rows_of(micro)
@@ -612,18 +626,20 @@
             moved(index)
 
     def forward_three(micro):
-        pair_wait(1)
-
-        def result(at, block, _):
-            stage[at] = middle[at] + pair_sum(1, block)
-
-        over_rows(micro, result)
+        for part in range(2):
+            pair(1, part).wait()
+
+            def result(at, block, _, part=part):
+                here = columns(part)
+                stage[at, here] = middle[at, here] + pair_part(1, part, block)
+
+            over_rows(micro, result)
+
+            @pl.when(section == 0)
+            def _(part=part):
+                leave_for(0, micro, part)
+
         output(0, micro).start()
-
-        @pl.when(section == 0)
-        def _():
-            pack(micro)
-            cross(0, micro).start()
 
     def norm_back(total, value, scale, gain):
         inner = total * gain
@@ -718,17 +734,18 @@
         LEFT_ORDER, ff, lambda i: (i, 2), own, place, left_finish, skipped=("x",)
     )
 
+    def mlp_grad(chunk, carry):
+        weight_grad(chunk, jnp.minimum(chunk // 3, 1), ff[chunk // 3, lax.rem(chunk, 3)].reshape(2 * ROW, CHUNK))
+        ring_start(chunk)
+        return carry
+
     def backward_one(micro):
         rows = rows_of(micro)
 
         @pl.when(section == 0)
         def _():
             arrive(1, micro)
-            cross(0, micro).wait_send()
-
-        @pl.when(section == 1)
-        def _():
-            load_cotangent(micro).wait()
+            cross_sent(0, micro)
 
         def hidden_back(chunk):
             wide[0] = dot(grad[rows], weight(DOWN + chunk))
@@ -752,20 +769,15 @@
             scaled = middle[rows, columns(part)] * scale_two[rows, :1]
             add_gains(8, part, jnp.sum(value * scaled, axis=0, keepdims=True))
 
-        def mlp_grad(chunk, carry):
-            weight_grad(chunk, jnp.minimum(chunk // 3, 1), ff[chunk // 3, lax.rem(chunk, 3)].reshape(2 * ROW, CHUNK))
-            ring_start(chunk)
-            return carry
-
         @pl.when(micro == 1)
         def _():
-            turn(0, grad)
-
             @pl.when(section == 0)
             def _():
+                turn(0, grad)
                 pl.semaphore_wait(s["left_free"], 2)
 
-            lax.fori_loop(DOWN, GATE, mlp_grad, 0)
+            lax.fori_loop(DOWN + 1, GATE, mlp_grad, 0)
+            mlp_grad(DOWN, 0)
 
         for index in range(2):
             normed_two_back(index)
@@ -776,14 +788,7 @@
             def _():
                 turn(1, normed_two)
 
-            lax.fori_loop(GATE, QUERY, mlp_grad, 0)
-
-            @pl.when(section == 1)
-            def _():
-                for device in (over_section, aslant):
-                    pl.semaphore_signal(
-                        s["left_free"], inc=1, device_id=device, device_id_type=MESH
-                    )
+            lax.fori_loop(GATE, jnp.where(section == 0, QUERY, SOON), mlp_grad, 0)
 
     def backward_two(micro):
         rows = rows_of(micro)
@@ -866,8 +871,20 @@
 
         @pl.when(section == 1)
         def _():
-            pack(micro)
-            cross(1, micro).start()
+            leave_for(1, micro, 0)
+            leave_for(1, micro, 1)
+
+        @pl.when((section == 1) & (micro == 1))
+        def _():
+            lax.fori_loop(SOON, QUERY, mlp_grad, 0)
+            for device in (over_section, aslant):
+                pl.semaphore_signal(s["left_free"], inc=1, device_id=device, device_id_type=MESH)
+
+    @pl.when(section == 1)
+    def _():
+        for micro in range(2):
+            load_cotangent(micro).wait()
+        turn(0, grad)
 
     def step(turn_of, carry):
         back = turn_of - 2 + section
@@ -950,7 +967,7 @@
 
         @pl.when(section == 1)
         def _(micro=micro):
-            cross(1, micro).wait_send()
+            cross_sent(1, micro)
 
 
 def rope_table():

time: 183 us -> 181 us (0.989)
  Pallas kernels: 176 us -> 174 us
    pallas_call x1, Pallas kernels: 173 us -> 170 us  [shards(): pl.pallas_call(kernel, out_shape=(full, full, jax.ShapeDtypeStruct((CHUNK...]
where the time goes in v5:
time: 181 us; the launch traced here: 180 us
  Pallas kernels  174 us (96%)
  local copies, waits for them, and re-layouts  5.08 us (3%)
    pallas_call x1, Pallas kernels, shards(): pl.pallas_call(kernel, out_shape=(full, full, jax.ShapeDtypeStruct((CHUNK...  170 us
    unnamed x8, local copies, waits for them, and re-layouts  5.08 us

profile of v5, /device:TPU:0, one launch (start us, length us, event | category | flops | bytes accessed | tf_op | source)
XLA Modules:
  0.0 179.5 jit_solution(11338694107684836428)
XLA Ops:
  0.7 170.3 %shard_map.246 = (f32[512,1024]{1,0:T(8,128)}, f32[512,1024]{1,0:T(8,128)}, f32[15,32,512]{2,1,0:T(8,128)}, f32[1,3072]{1,0:T(1,128)}) custom-call(s32[2,4]{1,0:T(2,128)} %lengths.1, bf16[512,1024]{1,0:T(8,128)(2,1)} %block_input.1, bf16[512,1024]{1,0:T(8,128)(2,1)} %cotangent.1, f32[1,1024]{1,0:T(1,128)} %attn_gain.1, f32[1,128]{1,0:T(1,128)} %q_gain.1, ...), custom_call_target="tpu_custom_call" | custom-call | tf_op jit(solution)/shard_map/pallas_call | solution.py:1014
  171.0 0.0 copy-start
  171.0 1.6 copy-done
  172.6 0.0 copy-start.1
  172.6 1.6 copy-done.1
  174.2 0.0 copy-start.2
  174.2 1.2 copy-done.2
  175.4 0.0 copy-start.3
  175.4 0.7 copy-done.3
  176.1 3.3 %shard_map.247 = (f32[1,512,1024]{2,1,0:T(8,128)}, f32[1,512,1024]{2,1,0:T(8,128)}, f32[1,1024]{1,0:T(1,128)}, f32[1,128]{1,0:T(1,128)}, f32[1,128]{1,0:T(1,128)...) custom-call(f32[512,1024]{1,0:T(8,128)S(1)} %copy-done, ...), custom_call_target="tpu_custom_call" | custom-call | tf_op jit(solution)/shard_map/pallas_call | solution.py:1088
Async XLA Ops:
  171.0 1.6 copy-start
  172.6 1.6 copy-start.1
  174.2 1.2 copy-start.2
  175.4 0.7 copy-start.3

commit v6 on v5

--- a/solution.py
+++ b/solution.py
@@ -760,24 +760,24 @@
 
             over_rows(micro, silu_back)
 
-        for index in range(3):
+        @pl.when((micro == 1) & (section == 0))
+        def _():
+            turn(0, grad)
+            pl.semaphore_wait(s["left_free"], 2)
+
+        for index in (1, 2, 0):
             hidden_back(index)
+
+            @pl.when(micro == 1)
+            def _(index=index):
+                mlp_grad(DOWN + index, 0)
+
 
         def normed_two_back(part):
             value = times_back(units(micro, 1, 2), range(GATE, QUERY), part)
             pair_start(2, part, value)
             scaled = middle[rows, columns(part)] * scale_two[rows, :1]
             add_gains(8, part, jnp.sum(value * scaled, axis=0, keepdims=True))
-
-        @pl.when(micro == 1)
-        def _():
-            @pl.when(section == 0)
-            def _():
-                turn(0, grad)
-                pl.semaphore_wait(s["left_free"], 2)
-
-            lax.fori_loop(DOWN + 1, GATE, mlp_grad, 0)
-            mlp_grad(DOWN, 0)
 
         for index in range(2):
             normed_two_back(index)

time: 181 us -> 181 us (level)
  no operation moved by 1% of the time
where the time goes in v6:
time: 181 us; the launch traced here: 180 us
  Pallas kernels  174 us (96%)
  local copies, waits for them, and re-layouts  5.08 us (3%)
    pallas_call x1, Pallas kernels, shards(): pl.pallas_call(kernel, out_shape=(full, full, jax.ShapeDtypeStruct((CHUNK...  171 us
    unnamed x8, local copies, waits for them, and re-layouts  5.08 us

profile of v6, /device:TPU:0, one launch (start us, length us, event | category | flops | bytes accessed | tf_op | source)
XLA Modules:
  0.0 180.1 jit_solution(3513801800865932899)
XLA Ops:
  0.7 170.9 %shard_map.246 = (f32[512,1024]{1,0:T(8,128)}, f32[512,1024]{1,0:T(8,128)}, f32[15,32,512]{2,1,0:T(8,128)}, f32[1,3072]{1,0:T(1,128)}) custom-call(s32[2,4]{1,0:T(2,128)} %lengths.1, bf16[512,1024]{1,0:T(8,128)(2,1)} %block_input.1, bf16[512,1024]{1,0:T(8,128)(2,1)} %cotangent.1, f32[1,1024]{1,0:T(1,128)} %attn_gain.1, f32[1,128]{1,0:T(1,128)} %q_gain.1, ...), custom_call_target="tpu_custom_call" | custom-call | tf_op jit(solution)/shard_map/pallas_call | solution.py:1014
  171.6 0.0 copy-start
  171.6 1.6 copy-done
  173.2 0.0 copy-start.1
  173.2 1.6 copy-done.1
  174.8 0.0 copy-start.2
  174.8 1.2 copy-done.2
  176.0 0.0 copy-start.3
  176.0 0.7 copy-done.3
  176.7 3.3 %shard_map.247 = (f32[1,512,1024]{2,1,0:T(8,128)}, f32[1,512,1024]{2,1,0:T(8,128)}, f32[1,1024]{1,0:T(1,128)}, f32[1,128]{1,0:T(1,128)}, f32[1,128]{1,0:T(1,128)...) custom-call(f32[512,1024]{1,0:T(8,128)S(1)} %copy-done, ...), custom_call_target="tpu_custom_call" | custom-call | tf_op jit(solution)/shard_map/pallas_call | solution.py:1088
Async XLA Ops:
  171.6 1.6 copy-start
  173.2 1.6 copy-start.1
  174.8 1.2 copy-start.2
  176.0 0.7 copy-start.3
